TPU v7x, 32 devices: a whole 2x2x4 slice. The times are simulated.
32 devices in a mesh: dp: 2 (over y), seq: 4 (over x, core), head: 4 (over z).
Axes of the slice: x: 2, y: 2, z: 4, core: 2. Of those that a mesh axis runs over, the one named last changes fastest.
Arguments:
- target: bfloat16 [4, 1024, 768], P('dp', 'seq'), may hold values from -6 to 6
- memory: bfloat16 [4, 6144, 768], P('dp', 'seq'), may hold values from -6 to 6
- memory_mark: int32 [4, 6144], P('dp'), may hold values from 0 to 1, as said below
- self_in: bfloat16 [768, 3, 768], P(None, None, 'head'), may hold values from -0.21875 to 0.21875
- self_in_bias: float32 [2, 768], P(None, 'head'), may hold values from -3 to 3
- self_out: bfloat16 [768, 768], P('head'), may hold values from -0.625 to 0.625
- cross_in: bfloat16 [768, 3, 768], P(None, None, 'head'), may hold values from -0.21875 to 0.21875
- cross_in_bias: float32 [2, 768], P(None, 'head'), may hold values from -3 to 3
- cross_out: bfloat16 [768, 768], P('head'), may hold values from -0.625 to 0.625
- ffn_up: bfloat16 [768, 3072], P(None, 'head'), may hold values from -0.21875 to 0.21875
- ffn_up_bias: float32 [3072], P('head'), may hold values from -3 to 3
- ffn_down: bfloat16 [3072, 768], P('head'), may hold values from -0.109375 to 0.109375
- out_biases: float32 [3, 768], replicated, may hold values from -3 to 3
- norm_gains: float32 [3, 768], replicated, may hold values from 0.5 to 1.5
- norm_biases: float32 [3, 768], replicated, may hold values from -1.25 to 1.25
- cotangent: bfloat16 [4, 1024, 768], P('dp', 'seq'), may hold values from -6 to 6
Outputs:
- layer_out: float32 [4, 1024, 768], P('dp', 'seq')
- target_grad: float32 [4, 1024, 768], P('dp', 'seq')
- memory_grad: float32 [4, 6144, 768], P('dp', ('seq', 'head'))
- self_in_grad: float32 [768, 3, 768], P('dp', None, 'head')
- self_in_bias_grad: float32 [2, 768], P(None, 'head')
- self_out_grad: float32 [768, 768], P('head', 'dp')
- cross_in_grad: float32 [768, 3, 768], P('dp', None, 'head')
- cross_in_bias_grad: float32 [2, 768], P(None, 'head')
- cross_out_grad: float32 [768, 768], P('head', 'dp')
- ffn_up_grad: float32 [768, 3072], P('dp', 'head')
- ffn_up_bias_grad: float32 [3072], P('head')
- ffn_down_grad: float32 [3072, 768], P('head', 'dp')
- out_biases_grad: float32 [3, 768], replicated
- norm_gains_grad: float32 [3, 768], replicated
- norm_biases_grad: float32 [3, 768], replicated
Inputs may be any that keep to these rules, and one draw needn't show every extreme that they name: `memory_mark`: every item has a 1 in each aligned block of 1536 memory rows.
All inputs are finite; a program needn't handle non-finite values.
Results may differ from a plain program's by a relative error of at most 0.025.
The roundings to bfloat16 on the way count: a program that leaves them out, or rounds other values in their place, can miss the bound.
Values may be sent and summed in bfloat16 or wider, within the bound.
No kernel may reach another device: no remote copies, remote signals or barrier semaphores. Data moves between devices by JAX's collectives and lax.ppermute only.
A program may use at most 128 MiB of HBM per device.

v0:
```python
import jax
import jax.numpy as jnp
from jax import lax
from jax.sharding import PartitionSpec as P

HEAD_DIM = 64


masked_score = -1e30
norm_epsilon = 1e-05


def key_block(key_count):
    block_rows = min(512, key_count)
    while key_count % block_rows:
        block_rows = block_rows // 2
    return block_rows


def split_heads(matrix):
    return matrix.reshape(matrix.shape[0], matrix.shape[1], matrix.shape[2] // HEAD_DIM, HEAD_DIM)


def layer_norm(matrix, gain, shift):
    center = matrix - jnp.mean(matrix, axis=-1, keepdims=True)
    spread = jnp.mean(center * center, axis=-1, keepdims=True)
    return center * lax.rsqrt(spread + norm_epsilon) * gain + shift


def exact_gelu(matrix):
    return jax.nn.gelu(matrix, approximate=False)


def causal(query_base, query_rows):

    def allowed(offset, block_rows):
        query_pos = query_base + lax.broadcasted_iota(jnp.int32, (query_rows, block_rows), 0)
        key_pos = offset + lax.broadcasted_iota(jnp.int32, (query_rows, block_rows), 1)
        return (query_pos >= key_pos)[None, None]

    return allowed


def marked(marks, key_base):

    def allowed(offset, block_rows):
        live = lax.dynamic_slice_in_dim(marks, key_base + offset, block_rows, 1) > 0
        return live[:, None, None, :]

    return allowed


def take_block(pair, offset, block_rows, local_width):
    block = lax.dynamic_slice_in_dim(pair, offset, block_rows, 1)
    return (split_heads(block[:, :, :local_width]), split_heads(block[:, :, local_width:]))


def block_scores(query_heads, key_heads, allowed, offset, block_rows):
    scores = jnp.einsum(
        "bqhe,bkhe->bhqk", query_heads, key_heads, preferred_element_type=jnp.float32
    )
    return jnp.where(allowed(offset, block_rows), scores, masked_score)


def attend_forward(queries, pair, allowed):
    batch_items, query_rows, local_width = queries.shape
    key_count = pair.shape[1]
    block_rows = key_block(key_count)
    offsets = jnp.arange(key_count // block_rows, dtype=jnp.int32) * block_rows
    query_heads = split_heads(queries)

    def first_pass(running, offset):
        running_max, running_sum = running
        key_heads, value_heads = take_block(pair, offset, block_rows, local_width)
        scores = block_scores(query_heads, key_heads, allowed, offset, block_rows)
        new_max = jnp.maximum(running_max, jnp.max(scores, axis=-1))
        running_sum = running_sum * jnp.exp(running_max - new_max) + jnp.sum(
            jnp.exp(scores - new_max[..., None]), axis=-1
        )
        return ((new_max, running_sum), None)

    extent = (batch_items, local_width // HEAD_DIM, query_rows)
    initial = (jnp.full(extent, masked_score, jnp.float32), jnp.zeros(extent, jnp.float32))
    (running_max, running_sum), _ = lax.scan(first_pass, initial, offsets)
    log_total = running_max + jnp.log(running_sum)

    def second_pass(accumulated, offset):
        key_heads, value_heads = take_block(pair, offset, block_rows, local_width)
        scores = block_scores(query_heads, key_heads, allowed, offset, block_rows)
        weights = jnp.exp(scores - log_total[..., None]).astype(jnp.bfloat16)
        return (
            accumulated
            + jnp.einsum(
                "bhqk,bkhe->bqhe", weights, value_heads, preferred_element_type=jnp.float32
            ),
            None,
        )

    accumulated = jnp.zeros(
        (batch_items, query_rows, local_width // HEAD_DIM, HEAD_DIM), jnp.float32
    )
    accumulated, _ = lax.scan(second_pass, accumulated, offsets)
    return (accumulated.reshape(batch_items, query_rows, local_width), log_total)


def attend_backward(queries, pair, log_total, grad_low, row_dots, allowed):
    batch_items, query_rows, local_width = queries.shape
    key_count = pair.shape[1]
    block_rows = key_block(key_count)
    offsets = jnp.arange(key_count // block_rows, dtype=jnp.int32) * block_rows
    query_heads = split_heads(queries)
    grad_heads = split_heads(grad_low)

    def block_step(running, offset):
        grad_queries, grad_pair = running
        key_heads, value_heads = take_block(pair, offset, block_rows, local_width)
        scores = block_scores(query_heads, key_heads, allowed, offset, block_rows)
        weights = jnp.exp(scores - log_total[..., None])
        grad_weights = jnp.einsum(
            "bqhe,bkhe->bhqk", grad_heads, value_heads, preferred_element_type=jnp.float32
        )
        grad_scores = (weights * (grad_weights - row_dots[..., None])).astype(jnp.bfloat16)
        grad_queries = grad_queries + jnp.einsum(
            "bhqk,bkhe->bqhe", grad_scores, key_heads, preferred_element_type=jnp.float32
        )
        grad_keys = jnp.einsum(
            "bhqk,bqhe->bkhe", grad_scores, query_heads, preferred_element_type=jnp.float32
        )
        grad_values = jnp.einsum(
            "bhqk,bqhe->bkhe",
            weights.astype(jnp.bfloat16),
            grad_heads,
            preferred_element_type=jnp.float32,
        )
        block_grad = jnp.concatenate(
            [
                grad_keys.reshape(batch_items, block_rows, local_width),
                grad_values.reshape(batch_items, block_rows, local_width),
            ],
            axis=2,
        )
        return (
            (grad_queries, lax.dynamic_update_slice_in_dim(grad_pair, block_grad, offset, 1)),
            None,
        )

    initial = (
        jnp.zeros((batch_items, query_rows, local_width // HEAD_DIM, HEAD_DIM), jnp.float32),
        jnp.zeros((batch_items, key_count, 2 * local_width), jnp.float32),
    )
    (grad_queries, grad_pair), _ = lax.scan(block_step, initial, offsets)
    return (grad_queries.reshape(batch_items, query_rows, local_width), grad_pair)


def row_dot(grad_low, attention):
    product = split_heads(grad_low.astype(jnp.float32)) * split_heads(attention)
    return jnp.transpose(jnp.sum(product, axis=-1), (0, 2, 1))


def head_total(matrix):
    return lax.psum(matrix, "head")


def head_grad_total(matrix):
    return lax.psum(matrix, "head")


def column_sums(matrix):
    return jnp.sum(matrix.astype(jnp.float32), axis=(0, 1))


def shards(
    target,
    memory,
    memory_mark,
    self_in,
    self_in_bias,
    self_out,
    cross_in,
    cross_in_bias,
    cross_out,
    ffn_up,
    ffn_up_bias,
    ffn_down,
    out_biases,
    norm_gains,
    norm_biases,
    cotangent,
):
    batch_items, target_rows, model_width = target.shape
    local_width = self_in.shape[2]
    memory_rows = memory.shape[1]
    seq_place = lax.axis_index("seq")
    projected = jnp.einsum("btd,dkh->btkh", target, self_in, preferred_element_type=jnp.float32)
    query_one = ((projected[:, :, 0] + self_in_bias[0]) * 0.125).astype(jnp.bfloat16)
    pair_one = jnp.concatenate(
        [
            projected[:, :, 1].astype(jnp.bfloat16),
            (projected[:, :, 2] + self_in_bias[1]).astype(jnp.bfloat16),
        ],
        axis=2,
    )
    pair_all = lax.all_gather(pair_one, "seq", axis=1, tiled=True)
    self_mask = causal(seq_place * target_rows, target_rows)
    attn_one, log_total_one = attend_forward(query_one, pair_all, self_mask)
    attn_one_low = attn_one.astype(jnp.bfloat16)
    out_one = (
        head_total(
            jnp.einsum("btk,kd->btd", attn_one_low, self_out, preferred_element_type=jnp.float32)
        )
        + out_biases[0]
    )
    sum_one = target.astype(jnp.float32) + out_one
    hidden_one, norm_pull_one = jax.vjp(layer_norm, sum_one, norm_gains[0], norm_biases[0])
    hidden_one_low = hidden_one.astype(jnp.bfloat16)
    query_two = (
        (
            jnp.einsum(
                "btd,dk->btk", hidden_one_low, cross_in[:, 0], preferred_element_type=jnp.float32
            )
            + cross_in_bias[0]
        )
        * 0.125
    ).astype(jnp.bfloat16)
    memory_proj = jnp.einsum(
        "bmd,dkh->bmkh", memory, cross_in[:, 1:], preferred_element_type=jnp.float32
    )
    pair_two = jnp.concatenate(
        [
            memory_proj[:, :, 0].astype(jnp.bfloat16),
            (memory_proj[:, :, 1] + cross_in_bias[1]).astype(jnp.bfloat16),
        ],
        axis=2,
    )
    pair_two_all = lax.all_gather(pair_two, "seq", axis=1, tiled=True)
    attn_two, log_total_two = attend_forward(query_two, pair_two_all, marked(memory_mark, 0))
    attn_two_low = attn_two.astype(jnp.bfloat16)
    out_two = (
        head_total(
            jnp.einsum("btk,kd->btd", attn_two_low, cross_out, preferred_element_type=jnp.float32)
        )
        + out_biases[1]
    )
    hidden_two, norm_pull_two = jax.vjp(
        layer_norm, hidden_one + out_two, norm_gains[1], norm_biases[1]
    )
    hidden_two_low = hidden_two.astype(jnp.bfloat16)
    pre_act = (
        jnp.einsum("btd,df->btf", hidden_two_low, ffn_up, preferred_element_type=jnp.float32)
        + ffn_up_bias
    )
    active, gelu_pull = jax.vjp(exact_gelu, pre_act)
    active_low = active.astype(jnp.bfloat16)
    out_three = (
        head_total(
            jnp.einsum("btf,fd->btd", active_low, ffn_down, preferred_element_type=jnp.float32)
        )
        + out_biases[2]
    )
    layer_out, norm_pull_three = jax.vjp(
        layer_norm, hidden_two + out_three, norm_gains[2], norm_biases[2]
    )
    grad_sum_three, gain_three, shift_three = norm_pull_three(cotangent.astype(jnp.float32))
    grad_out_three = grad_sum_three.astype(jnp.bfloat16)
    down_grad = jnp.einsum(
        "btf,btd->fd", active_low, grad_out_three, preferred_element_type=jnp.float32
    )
    grad_active = jnp.einsum(
        "btd,fd->btf", grad_out_three, ffn_down, preferred_element_type=jnp.float32
    )
    (grad_pre,) = gelu_pull(grad_active)
    grad_pre_low = grad_pre.astype(jnp.bfloat16)
    up_grad = jnp.einsum(
        "btd,btf->df", hidden_two_low, grad_pre_low, preferred_element_type=jnp.float32
    )
    grad_hidden_two = grad_sum_three + head_grad_total(
        jnp.einsum("btf,df->btd", grad_pre_low, ffn_up, preferred_element_type=jnp.float32)
    )
    grad_sum_two, gain_two, shift_two = norm_pull_two(grad_hidden_two)
    grad_out_two = grad_sum_two.astype(jnp.bfloat16)
    cross_out_grad = jnp.einsum(
        "btk,btd->kd", attn_two_low, grad_out_two, preferred_element_type=jnp.float32
    )
    grad_attn_two = jnp.einsum(
        "btd,kd->btk", grad_out_two, cross_out, preferred_element_type=jnp.float32
    ).astype(jnp.bfloat16)
    cross_dot = row_dot(grad_attn_two, attn_two)
    grad_query_two, grad_pair_whole = attend_backward(
        query_two, pair_two_all, log_total_two, grad_attn_two, cross_dot, marked(memory_mark, 0)
    )
    grad_pair_two = lax.psum_scatter(grad_pair_whole, "seq", scatter_dimension=1, tiled=True)
    grad_query_two_low = grad_query_two.astype(jnp.bfloat16) * 0.125
    grad_memory_low = grad_pair_two.astype(jnp.bfloat16).reshape(
        batch_items, memory_rows, 2, local_width
    )
    query_weight_two = jnp.einsum(
        "btd,btk->dk", hidden_one_low, grad_query_two_low, preferred_element_type=jnp.float32
    )
    memory_weight_two = jnp.einsum(
        "bmd,bmkh->dkh", memory, grad_memory_low, preferred_element_type=jnp.float32
    )
    cross_in_grad = jnp.concatenate([query_weight_two[:, None], memory_weight_two], axis=1)
    cross_bias_grad = jnp.stack(
        [column_sums(grad_query_two_low), column_sums(grad_memory_low[:, :, 1])]
    )
    memory_part = jnp.einsum(
        "bmkh,dkh->bmd", grad_memory_low, cross_in[:, 1:], preferred_element_type=jnp.float32
    )
    memory_grad = lax.psum_scatter(memory_part, "head", scatter_dimension=1, tiled=True)
    grad_hidden_one = grad_sum_two + head_grad_total(
        jnp.einsum(
            "btk,dk->btd", grad_query_two_low, cross_in[:, 0], preferred_element_type=jnp.float32
        )
    )
    grad_sum_one, gain_one, shift_one = norm_pull_one(grad_hidden_one)
    grad_out_one = grad_sum_one.astype(jnp.bfloat16)
    self_out_grad = jnp.einsum(
        "btk,btd->kd", attn_one_low, grad_out_one, preferred_element_type=jnp.float32
    )
    grad_attn_one = jnp.einsum(
        "btd,kd->btk", grad_out_one, self_out, preferred_element_type=jnp.float32
    ).astype(jnp.bfloat16)
    self_dot = row_dot(grad_attn_one, attn_one)
    grad_query_one, grad_pair_whole_one = attend_backward(
        query_one, pair_all, log_total_one, grad_attn_one, self_dot, self_mask
    )
    grad_pair_one = lax.psum_scatter(
        grad_pair_whole_one, "seq", scatter_dimension=1, tiled=True
    ).astype(jnp.bfloat16)
    grad_proj = jnp.concatenate(
        [
            (grad_query_one.astype(jnp.bfloat16) * 0.125)[:, :, None],
            grad_pair_one.reshape(batch_items, target_rows, 2, local_width),
        ],
        axis=2,
    )
    self_in_grad = jnp.einsum(
        "btd,btkh->dkh", target, grad_proj, preferred_element_type=jnp.float32
    )
    self_bias_grad = jnp.stack([column_sums(grad_proj[:, :, 0]), column_sums(grad_proj[:, :, 2])])
    target_grad = grad_sum_one + head_grad_total(
        jnp.einsum("btkh,dkh->btd", grad_proj, self_in, preferred_element_type=jnp.float32)
    )
    row_shares = (
        lax.psum_scatter(self_in_grad, "dp", scatter_dimension=0, tiled=True),
        lax.psum_scatter(cross_in_grad, "dp", scatter_dimension=0, tiled=True),
        lax.psum_scatter(up_grad, "dp", scatter_dimension=0, tiled=True),
    )
    column_shares = (
        lax.psum_scatter(self_out_grad, "dp", scatter_dimension=1, tiled=True),
        lax.psum_scatter(cross_out_grad, "dp", scatter_dimension=1, tiled=True),
        lax.psum_scatter(down_grad, "dp", scatter_dimension=1, tiled=True),
    )
    seq_totals = lax.psum(
        (
            row_shares[0],
            row_shares[1],
            row_shares[2],
            column_shares[0],
            column_shares[1],
            column_shares[2],
        ),
        "seq",
    )
    out_bias_grad = jnp.stack(
        [column_sums(grad_out_one), column_sums(grad_out_two), column_sums(grad_out_three)]
    )
    small_totals = lax.psum(
        (
            self_bias_grad,
            cross_bias_grad,
            column_sums(grad_pre_low),
            out_bias_grad,
            jnp.stack([gain_one, gain_two, gain_three]),
            jnp.stack([shift_one, shift_two, shift_three]),
        ),
        ("dp", "seq"),
    )
    return (
        layer_out,
        target_grad,
        memory_grad,
        seq_totals[0],
        small_totals[0],
        seq_totals[3],
        seq_totals[1],
        small_totals[1],
        seq_totals[4],
        seq_totals[2],
        small_totals[2],
        seq_totals[5],
        small_totals[3],
        small_totals[4],
        small_totals[5],
    )


def solution(mesh):
    return jax.shard_map(
        shards,
        mesh=mesh,
        in_specs=(
            P("dp", "seq", None),
            P("dp", "seq", None),
            P("dp", None),
            P(None, None, "head"),
            P(None, "head"),
            P("head", None),
            P(None, None, "head"),
            P(None, "head"),
            P("head", None),
            P(None, "head"),
            P("head"),
            P("head", None),
            P(),
            P(),
            P(),
            P("dp", "seq", None),
        ),
        out_specs=(
            P("dp", "seq", None),
            P("dp", "seq", None),
            P("dp", ("seq", "head"), None),
            P("dp", None, "head"),
            P(None, "head"),
            P("head", "dp"),
            P("dp", None, "head"),
            P(None, "head"),
            P("head", "dp"),
            P("dp", "head"),
            P("head"),
            P("head", "dp"),
            P(),
            P(),
            P(),
        ),
        check_vma=False,
    )
```

profile of v0, /device:TPU:9, one launch (start us, length us, event | category | flops | bytes accessed | tf_op | source)
XLA Modules:
  0.0 1685.3 jit_solution(11901919486222981494)
XLA Ops:
  12.9 6.6 fusion.41
  19.5 13.1 all-gather.3.cloned.1.call-done
  32.6 12.9 while.74
  45.6 15.7 while.75
  71.0 60.4 %all-reduce.10.cloned.1.call-done = f32[2,256,768]{2,1,0:T(8,128)} async-done(((f32[2,256,768]{2,1,0:T(8,128)}), f32[2,256,768]{2,1,0:T(8,128)}) %all-reduce.10.cloned.1.call-update) | async-done | bytes 1572880 | tf_op jit(solution)/shard_map/psum | solution.py:161
  136.5 61.9 %all-gather.5.cloned.1.call-done = bf16[2,6144,384]{1,2,0:T(8,128)(2,1)} async-done(((bf16[2,1536,384]{1,2,0:T(8,128)(2,1)}), bf16[2,6144,384]{1,2,0:T(8,128)(2,1)}) %all-gather.5.cloned.1.call-update) | async-done | bytes 9437200 | tf_op jit(solution)/shard_map/all_gather | solution.py:235
  198.4 81.1 %while.76 = (s32[]{:T(128)}, f32[2,3,256]{2,1,0:T(4,128)S(1)}, f32[2,3,256]{2,1,0:T(4,128)S(1)}, s32[12]{0:T(128)}, s32[2,6144]{1,0:T(2,128)}, /*index=5*/bf16[2...) while((s32[]{:T(128)}, f32[2,3,256]{2,1,0:T(4,128)S(1)}, ...), condition=%wide.region_12.13_spmd.clone, body=%wide.region_9.12_spmd.clone.sunk | while | flops 104604160 | bytes 7754926 | solution.py:84
  279.6 119.9 %while.77 = (s32[]{:T(128)}, f32[2,256,3,64]{1,3,2,0:T(8,128)}, s32[12]{0:T(128)}, bf16[2,6144,384]{1,2,0:T(8,128)(2,1)}, s32[2,6144]{1,0:T(2,128)}, /*index=5*/...) while((s32[]{:T(128)}, f32[2,256,3,64]{1,3,2,0:T(8,128)}, ...), condition=%wide.region_14.15_spmd.clone, body=%wide.region_13.14_spmd.clone.sunk | while | flops 203883520 | bytes 3354821 | solution.py:102
  296.3 3.2 fusion.221
  316.3 3.2 fusion.221
  403.5 67.4 %all-reduce.12.cloned.1.call-done = f32[2,256,768]{2,1,0:T(8,128)} async-done(((f32[2,256,768]{2,1,0:T(8,128)}), f32[2,256,768]{2,1,0:T(8,128)}) %all-reduce.12.cloned.1.call-update) | async-done | bytes 1572880 | tf_op jit(solution)/shard_map/psum | solution.py:161
  474.9 4.5 multiply_convert_fusion.1
  481.4 68.3 %all-reduce.14.cloned.1.call-done = f32[2,256,768]{2,1,0:T(8,128)} async-done(((f32[2,256,768]{2,1,0:T(8,128)}), f32[2,256,768]{2,1,0:T(8,128)}) %all-reduce.14.cloned.1.call-update) | async-done | bytes 1572880 | tf_op jit(solution)/shard_map/psum | solution.py:161
  561.4 68.3 %all-reduce.16.cloned.1.call-done = f32[2,256,768]{2,1,0:T(8,128)} async-done(((f32[2,256,768]{2,1,0:T(8,128)}), f32[2,256,768]{2,1,0:T(8,128)}) %all-reduce.16.cloned.1.call-update) | async-done | bytes 1572880 | tf_op jit(solution)/shard_map/psum | solution.py:165
  629.7 4.5 multiply_reduce_fusion
  637.1 8.8 broadcast_in_dim.109
  645.9 225.3 %while.78 = (s32[]{:T(128)}, f32[2,256,3,64]{1,3,2,0:T(8,128)S(1)}, f32[2,6144,384]{1,2,0:T(8,128)}, s32[12]{0:T(128)}, bf16[2,6144,384]{1,2,0:T(8,128)(2,1)}, /...) while((s32[]{:T(128)}, f32[2,256,3,64]{1,3,2,0:T(8,128)S(1)}, ...), condition=%wide.region_28.29_spmd.clone, body=%wide.region_27.28_spmd.clone.sunk | while | flops 510198784 | bytes 26371296 | solution.py:151
  656.6 8.2 dynamic_update_slice.10
  675.4 8.3 dynamic_update_slice.10
  694.3 8.2 dynamic_update_slice.10
  713.1 8.2 dynamic_update_slice.10
  731.9 8.2 dynamic_update_slice.10
  750.8 8.2 dynamic_update_slice.10
  769.7 8.3 dynamic_update_slice.10
  788.6 8.2 dynamic_update_slice.10
  807.4 8.2 dynamic_update_slice.10
  826.3 8.2 dynamic_update_slice.10
  845.1 8.2 dynamic_update_slice.10
  863.9 7.3 dynamic_update_slice.10
  874.8 68.1 %all-reduce.18.cloned.1.call-done = f32[2,256,768]{2,1,0:T(8,128)} async-done(((f32[2,256,768]{2,1,0:T(8,128)}), f32[2,256,768]{2,1,0:T(8,128)}) %all-reduce.18.cloned.1.call-update) | async-done | bytes 1572880 | tf_op jit(solution)/shard_map/psum | solution.py:165
  942.9 3.3 multiply_reduce_fusion.1
  951.2 35.3 %while.79 = (s32[]{:T(128)}, f32[2,256,3,64]{1,3,2,0:T(8,128)S(1)}, f32[2,1024,384]{1,2,0:T(8,128)}, s32[2]{0:T(128)}, bf16[2,1024,384]{1,2,0:T(8,128)(2,1)}, /*...) while((s32[]{:T(128)}, f32[2,256,3,64]{1,3,2,0:T(8,128)S(1)}, ...), condition=%wide.region_34.35_spmd.clone, body=%wide.region_33.34_spmd.clone.sunk | while | flops 510329600 | bytes 26763492 | solution.py:151
  961.2 8.2 dynamic_update_slice.11
  979.2 7.3 dynamic_update_slice.11
  998.0 26.8 %reduce-scatter.10.cloned.1.call-done = f32[2,256,384]{1,2,0:T(8,128)} async-done(((f32[2,1024,384]{1,2,0:T(8,128)}), f32[2,256,384]{1,2,0:T(8,128)}) %reduce-scatter.10.cloned.1.call-update) | async-done | bytes 786448 | tf_op jit(solution)/shard_map/reduce_scatter | solution.py:327
  1029.8 137.3 %reduce-scatter.12.cloned.1.call-done = f32[2,1536,384]{1,2,0:T(8,128)} async-done(((f32[2,6144,384]{1,2,0:T(8,128)}), f32[2,1536,384]{1,2,0:T(8,128)}) %reduce-scatter.12.cloned.1.call-update) | async-done | bytes 4718608 | tf_op jit(solution)/shard_map/reduce_scatter | solution.py:291
  1169.7 5.2 fusion.55
  1179.5 5.0 reduce-scatter.22.cloned.1.call-done
  1184.5 18.2 %reduce-scatter.18.cloned.1.call-done = f32[192,384]{1,0:T(8,128)} async-done(((f32[192,768]{1,0:T(8,128)}), f32[192,384]{1,0:T(8,128)}) %reduce-scatter.18.cloned.1.call-update) | async-done | bytes 294928 | tf_op jit(solution)/shard_map/reduce_scatter | solution.py:350
  1202.8 37.4 %reduce-scatter.24.cloned.1.call-done = f32[384,768]{1,0:T(8,128)} async-done(((f32[768,768]{1,0:T(8,128)}), f32[384,768]{1,0:T(8,128)}) %reduce-scatter.24.cloned.1.call-update) | async-done | bytes 1179664 | tf_op jit(solution)/shard_map/reduce_scatter | solution.py:347
  1240.2 37.0 %reduce-scatter.26.cloned.1.call-done = f32[768,384]{1,0:T(8,128)} async-done(((f32[768,768]{1,0:T(8,128)}), f32[768,384]{1,0:T(8,128)}) %reduce-scatter.26.cloned.1.call-update) | async-done | bytes 1179664 | tf_op jit(solution)/shard_map/reduce_scatter | solution.py:352
  1277.2 30.4 %reduce-scatter.16.cloned.1.call-done = f32[384,3,192]{0,2,1:T(8,128)} async-done(((f32[768,3,192]{0,2,1:T(8,128)}), f32[384,3,192]{0,2,1:T(8,128)}) %reduce-scatter.16.cloned.1.call-update) | async-done | bytes 884752 | tf_op jit(solution)/shard_map/reduce_scatter | solution.py:345
  1307.6 30.5 %reduce-scatter.20.cloned.1.call-done = f32[384,3,192]{0,2,1:T(8,128)} async-done(((f32[768,3,192]{0,2,1:T(8,128)}), f32[384,3,192]{0,2,1:T(8,128)}) %reduce-scatter.20.cloned.1.call-update) | async-done | bytes 884752 | tf_op jit(solution)/shard_map/reduce_scatter | solution.py:346
  1339.3 7.9 convolution_bitcast_fusion.2
  1348.4 60.6 %all-reduce.20.cloned.1.call-done = f32[2,256,768]{2,1,0:T(8,128)} async-done(((f32[2,256,768]{2,1,0:T(8,128)}), f32[2,256,768]{2,1,0:T(8,128)}) %all-reduce.20.cloned.1.call-update) | async-done | bytes 1572880 | tf_op jit(solution)/shard_map/psum | solution.py:165
  1412.2 23.4 %all-reduce = (f32[2,192]{1,0:T(2,128)}, f32[2,192]{1,0:T(2,128)}, f32[768]{0:T(1024)}, f32[3,768]{1,0:T(4,128)}, f32[3,768]{1,0:T(4,128)}, /*index=5*/f32[3,768]{1,0:T(4,128)}) all-reduce(f32[2,192]{1,0:T(2,128)S(1)} %pad_maximum_fusion.11, ...), channel_id=1, replica_groups=mesh['dp'=2,'seq'=4,'head'=4] {'dp','seq'}, use_global_device_ids=true, to_apply=%region_43.44 | all-reduce | flops 8448 | bytes 67584 | tf_op jit(solution)/shard_map/psum | solution.py:368
  1435.5 71.8 %all-reduce.22.cloned.1.call-done = (f32[384,3,192]{0,2,1:T(8,128)}, f32[192,384]{1,0:T(8,128)}, f32[384,3,192]{0,2,1:T(8,128)}, f32[192,384]{1,0:T(8,128)}, f32[384,768]{1,0:T(8,128)}, /*index=5*/f32[768,384]{1,0:T(8,128)}) async-done(((f32[384,3,192]{0,2,1:T(8,128)}, f32[192,384]{1,0:T(8,128)}, f32[384,3,192]{0,2,1:T(8,128)}, f32[192,384]{1,0:T(8,128)}, f32[384,768]{1,0:T(8,128)}, ...) | async-done | bytes 4718608 | tf_op jit(solution)/shard_map/psum | solution.py:354
  1507.4 164.3 %reduce-scatter.14.cloned.1.call-done = f32[2,384,768]{2,1,0:T(8,128)} async-done(((f32[2,1536,768]{2,1,0:T(8,128)}), f32[2,384,768]{2,1,0:T(8,128)}) %reduce-scatter.14.cloned.1.call-update) | async-done | bytes 2359312 | tf_op jit(solution)/shard_map/reduce_scatter | solution.py:309
  (627 shorter events, 374.3 us)
Async XLA Ops:
  7.2 466.1 %copy-start = (bf16[768,768]{1,0:T(8,128)(2,1)S(1)}, bf16[768,768]{1,0:T(8,128)(2,1)}, u32[]{:S(2)}) copy-start(bf16[768,768]{1,0:T(8,128)(2,1)} %param.37) | copy-start | bytes 3538948
  7.2 25.4 %all-gather.3.cloned.1.call-start = ((), (), s32[]{:S(2)}) async-start(), calls=%async_computation.9 | async-start | bytes 1966080 | tf_op jit(solution)/shard_map/all_gather | solution.py:203
  11.0 120.4 %all-reduce.10.cloned.1.call-start = ((), (), s32[]{:S(2)}) async-start(), calls=%async_computation.10 | async-start | bytes 3145728 | tf_op jit(solution)/shard_map/psum | solution.py:161
  45.5 16.5 copy-start.30
  63.7 134.8 %all-gather.5.cloned.1.call-start = ((), (), s32[]{:S(2)}) async-start(), calls=%async_computation.11 | async-start | bytes 11796480 | tf_op jit(solution)/shard_map/all_gather | solution.py:235
  69.1 401.8 %all-reduce.12.cloned.1.call-start = ((), (), s32[]{:S(2)}) async-start(), calls=%async_computation.12 | async-start | bytes 3145728 | tf_op jit(solution)/shard_map/psum | solution.py:161
  70.4 63.3 %copy-start.56 = (f32[768]{0:T(1024)}, f32[768]{0:T(1024)S(1)}, u32[]{:S(2)}) copy-start(f32[768]{0:T(1024)S(1)} %get-tuple-element.474) | copy-start | bytes 9220
  71.0 62.7 %copy-start.41 = (f32[768]{0:T(1024)}, f32[768]{0:T(1024)S(1)}, u32[]{:S(2)}) copy-start(f32[768]{0:T(1024)S(1)} %get-tuple-element.471) | copy-start | bytes 9220
  133.3 337.5 %copy-start.2 = (f32[2,256,768]{2,1,0:T(8,128)}, f32[2,256,768]{2,1,0:T(8,128)S(1)}, u32[]{:S(2)}) copy-start(f32[2,256,768]{2,1,0:T(8,128)S(1)} %get-tuple-element.610) | copy-start | bytes 4718596
  400.5 70.4 %copy-start.42 = (f32[768]{0:T(1024)S(1)}, f32[768]{0:T(1024)}, u32[]{:S(2)}) copy-start(f32[768]{0:T(1024)} %copy-done.41) | copy-start | bytes 9220
  400.5 70.4 %copy-start.46 = (f32[2,256]{1,0:T(2,128)S(1)}, f32[2,256]{1,0:T(2,128)}, u32[]{:S(2)}) copy-start(f32[2,256]{1,0:T(2,128)} %copy-done.45) | copy-start | bytes 6148
  400.5 70.4 %copy-start.51 = (f32[2,256]{1,0:T(2,128)S(1)}, f32[2,256]{1,0:T(2,128)}, u32[]{:S(2)}) copy-start(f32[2,256]{1,0:T(2,128)} %copy-done.50) | copy-start | bytes 6148
  400.5 70.4 %copy-start.57 = (f32[768]{0:T(1024)S(1)}, f32[768]{0:T(1024)}, u32[]{:S(2)}) copy-start(f32[768]{0:T(1024)} %copy-done.56) | copy-start | bytes 9220
  400.5 70.4 %copy-start.80 = (f32[768]{0:T(1024)S(1)}, f32[768]{0:T(1024)}, u32[]{:S(2)}) copy-start(f32[768]{0:T(1024)} %get-tuple-element.633) | copy-start | bytes 9220
  403.1 146.6 %all-reduce.14.cloned.1.call-start = ((), (), s32[]{:S(2)}) async-start(), calls=%async_computation.13 | async-start | bytes 3145728 | tf_op jit(solution)/shard_map/psum | solution.py:161
  472.9 161.3 %copy-start.54 = (f32[2,256]{1,0:T(2,128)}, f32[2,256]{1,0:T(2,128)S(1)}, u32[]{:S(2)}) copy-start(f32[2,256]{1,0:T(2,128)S(1)} %broadcast_multiply_fusion.1) | copy-start | bytes 6148
  473.3 160.9 %copy-start.59 = (f32[2,256]{1,0:T(2,128)}, f32[2,256]{1,0:T(2,128)S(1)}, u32[]{:S(2)}) copy-start(f32[2,256]{1,0:T(2,128)S(1)} %fusion.99) | copy-start | bytes 6148
  481.3 68.3 %copy-start.79 = (f32[768]{0:T(1024)S(1)}, f32[768]{0:T(1024)}, u32[]{:S(2)}) copy-start(f32[768]{0:T(1024)} %get-tuple-element.635) | copy-start | bytes 9220
  481.4 148.3 %all-reduce.16.cloned.1.call-start = ((), (), s32[]{:S(2)}) async-start(), calls=%async_computation.14 | async-start | bytes 3145728 | tf_op jit(solution)/shard_map/psum | solution.py:165
  561.3 68.4 %copy-start.12 = (bf16[2,256,768]{2,1,0:T(8,128)(2,1)S(1)}, bf16[2,256,768]{2,1,0:T(8,128)(2,1)}, u32[]{:S(2)}) copy-start(bf16[2,256,768]{2,1,0:T(8,128)(2,1)} %param.43) | copy-start | bytes 2359300
  561.3 68.4 %copy-start.74 = (f32[768]{0:T(1024)S(1)}, f32[768]{0:T(1024)}, u32[]{:S(2)}) copy-start(f32[768]{0:T(1024)} %get-tuple-element.473) | copy-start | bytes 9220
  561.4 381.5 %all-reduce.18.cloned.1.call-start = ((), (), s32[]{:S(2)}) async-start(), calls=%async_computation.15 | async-start | bytes 3145728 | tf_op jit(solution)/shard_map/psum | solution.py:165
  629.7 4.5 copy-start.6
  635.6 10.3 copy-start.13
  871.9 71.0 %copy-start.3 = (f32[2,256,768]{2,1,0:T(8,128)S(1)}, f32[2,256,768]{2,1,0:T(8,128)}, u32[]{:S(2)}) copy-start(f32[2,256,768]{2,1,0:T(8,128)} %copy-done.2) | copy-start | bytes 4718596
  871.9 71.0 %copy-start.43 = (f32[768]{0:T(1024)S(1)}, f32[768]{0:T(1024)}, u32[]{:S(2)}) copy-start(f32[768]{0:T(1024)} %copy-done.41) | copy-start | bytes 9220
  871.9 71.0 %copy-start.47 = (f32[2,256]{1,0:T(2,128)S(1)}, f32[2,256]{1,0:T(2,128)}, u32[]{:S(2)}) copy-start(f32[2,256]{1,0:T(2,128)} %copy-done.45) | copy-start | bytes 6148
  871.9 71.0 %copy-start.52 = (f32[2,256]{1,0:T(2,128)S(1)}, f32[2,256]{1,0:T(2,128)}, u32[]{:S(2)}) copy-start(f32[2,256]{1,0:T(2,128)} %copy-done.50) | copy-start | bytes 6148
  871.9 71.0 %copy-start.66 = (f32[2,256]{1,0:T(2,128)S(1)}, f32[2,256]{1,0:T(2,128)}, u32[]{:S(2)}) copy-start(f32[2,256]{1,0:T(2,128)} %copy-done.65) | copy-start | bytes 6148
  874.6 150.2 %reduce-scatter.10.cloned.1.call-start = ((), (), s32[]{:S(2)}) async-start(), calls=%async_computation.16 | async-start | bytes 3932160 | tf_op jit(solution)/shard_map/reduce_scatter | solution.py:327
  874.8 71.4 %copy-start.62 = (f32[2,256]{1,0:T(2,128)S(1)}, f32[2,256]{1,0:T(2,128)}, u32[]{:S(2)}) copy-start(f32[2,256]{1,0:T(2,128)} %copy-done.61) | copy-start | bytes 6148
  986.6 180.5 %reduce-scatter.12.cloned.1.call-start = ((), (), s32[]{:S(2)}) async-start(), calls=%async_computation.18 | async-start | bytes 23592960 | tf_op jit(solution)/shard_map/reduce_scatter | solution.py:291
  987.3 197.2 %reduce-scatter.22.cloned.1.call-start = ((), (), s32[]{:S(2)}) async-start(), calls=%async_computation.23 | async-start | bytes 884736 | tf_op jit(solution)/shard_map/reduce_scatter | solution.py:351
  989.0 213.8 %reduce-scatter.18.cloned.1.call-start = ((), (), s32[]{:S(2)}) async-start(), calls=%async_computation.21 | async-start | bytes 884736 | tf_op jit(solution)/shard_map/reduce_scatter | solution.py:350
  991.5 248.7 %reduce-scatter.24.cloned.1.call-start = ((), (), s32[]{:S(2)}) async-start(), calls=%async_computation.24 | async-start | bytes 3538944 | tf_op jit(solution)/shard_map/reduce_scatter | solution.py:347
  994.0 283.2 %reduce-scatter.26.cloned.1.call-start = ((), (), s32[]{:S(2)}) async-start(), calls=%async_computation.25 | async-start | bytes 3538944 | tf_op jit(solution)/shard_map/reduce_scatter | solution.py:352
  997.8 28.1 %copy-start.16 = (bf16[2,256,768]{2,1,0:T(8,128)(2,1)S(1)}, bf16[2,256,768]{2,1,0:T(8,128)(2,1)}, u32[]{:S(2)}) copy-start(bf16[2,256,768]{2,1,0:T(8,128)(2,1)} %param.28) | copy-start | bytes 2359300
  997.8 309.8 %reduce-scatter.16.cloned.1.call-start = ((), (), s32[]{:S(2)}) async-start(), calls=%async_computation.20 | async-start | bytes 2654208 | tf_op jit(solution)/shard_map/reduce_scatter | solution.py:345
  1027.9 310.2 %reduce-scatter.20.cloned.1.call-start = ((), (), s32[]{:S(2)}) async-start(), calls=%async_computation.22 | async-start | bytes 2654208 | tf_op jit(solution)/shard_map/reduce_scatter | solution.py:346
  1169.7 5.2 copy-start.17
  1176.3 232.7 %all-reduce.20.cloned.1.call-start = ((), (), s32[]{:S(2)}) async-start(), calls=%async_computation.17 | async-start | bytes 3145728 | tf_op jit(solution)/shard_map/psum | solution.py:165
  1179.4 328.0 %all-reduce.22.cloned.1.call-start = ((), (), s32[]{:S(2)}) async-start(), calls=%async_computation.26 | async-start | bytes 9437184 | tf_op jit(solution)/shard_map/psum | solution.py:354
  1338.1 333.6 %reduce-scatter.14.cloned.1.call-start = ((), (), s32[]{:S(2)}) async-start(), calls=%async_computation.19 | async-start | bytes 11796480 | tf_op jit(solution)/shard_map/reduce_scatter | solution.py:309
  1347.3 61.7 %copy-start.9 = (f32[2,256,768]{2,1,0:T(8,128)S(1)}, f32[2,256,768]{2,1,0:T(8,128)}, u32[]{:S(2)}) copy-start(f32[2,256,768]{2,1,0:T(8,128)} %copy-done.8) | copy-start | bytes 4718596
  1347.3 61.7 %copy-start.64 = (f32[2,256]{1,0:T(2,128)S(1)}, f32[2,256]{1,0:T(2,128)}, u32[]{:S(2)}) copy-start(f32[2,256]{1,0:T(2,128)} %copy-done.63) | copy-start | bytes 6148
  1348.4 63.8 %copy-start.85 = (f32[768]{0:T(1024)S(1)}, f32[768]{0:T(1024)}, u32[]{:S(2)}) copy-start(f32[768]{0:T(1024)} %get-tuple-element.631) | copy-start | bytes 9220
  1507.4 166.5 %copy-start.39 = (f32[192,384]{1,0:T(8,128)S(1)}, f32[192,384]{1,0:T(8,128)}, u32[]{:S(2)}) copy-start(f32[192,384]{1,0:T(8,128)} %get-tuple-element.1169) | copy-start | bytes 884740
  1507.4 167.2 %copy-start.33 = (f32[384,3,192]{0,2,1:T(8,128)S(1)}, f32[384,3,192]{0,2,1:T(8,128)}, u32[]{:S(2)}) copy-start(f32[384,3,192]{0,2,1:T(8,128)} %get-tuple-element.1170) | copy-start | bytes 2654212
  (62 other events, 107.1 us)
Sparse Core Ops, SparseCore 0:
  11.2 21.4 all-gather.2
  63.8 67.6 all-reduce.9
  133.6 64.7 all-gather.4
  403.2 67.6 all-reduce.11
  481.5 68.1 all-reduce.13
  561.5 68.1 all-reduce.15
  874.7 68.1 all-reduce.17
  986.7 38.0 reduce-scatter.9
  1027.6 139.4 reduce-scatter.11
  1169.2 15.2 reduce-scatter.21
  1187.5 15.2 reduce-scatter.17
  1205.4 34.7 reduce-scatter.23
  1242.5 34.6 reduce-scatter.25
  1279.3 28.2 reduce-scatter.15
  1309.8 28.2 reduce-scatter.19
  1340.9 68.0 all-reduce.19
  1411.6 95.7 all-reduce.21
  1510.2 161.5 reduce-scatter.13
where the time goes:
time: 1700 us; the launch traced here: 1690 us
  waiting for transfers between devices  1030 us (61%)
  local copies, waits for them, and re-layouts  269 us (16%)
  matrix products  170 us (10%)
  other arithmetic  93.2 us (5%)
  loops' own time  84.8 us (5%)
  blocking collectives  23.4 us (1%)
    psum x3, waiting for transfers between devices, head_grad_total(): return lax.psum(matrix, 'head')  197 us
    psum x3, waiting for transfers between devices, head_total(): return lax.psum(matrix, 'head')  196 us
    reduce_scatter x1, waiting for transfers between devices, shards(): lax.psum_scatter(memory_part, 'head', scatter_dimension=1, tiled=True)  164 us
    reduce_scatter x1, waiting for transfers between devices, shards(): lax.psum_scatter(grad_pair_whole, 'seq', scatter_dimension=1, tiled=True)  137 us
    dynamic_update_slice x14, local copies, waits for them, and re-layouts, block_step(): lax.dynamic_update_slice_in_dim(grad_pair, block_grad, offset, 1)  113 us
    psum x1, waiting for transfers between devices, shards(): lax.psum((row_shares[0], row_shares[1], row_shares[2], column_shares[0],...  71.8 us
    all_gather x1, waiting for transfers between devices, shards(): pair_two_all = lax.all_gather(pair_two, 'seq', axis=1, tiled=True)  61.9 us
    dynamic_slice x42, local copies, waits for them, and re-layouts, attend_forward(): (running_max, running_sum), _ = lax.scan(first_pass, initial, offsets)  53.2 us
  transfers between devices with their start and end apart: 18, of which 18 were waited for; matrix products, arithmetic and copies ran while one was open for 3% of the time, Pallas kernels for 0%

commit v1 on v0

v1 whole, which is shorter than its diff:
```python
import jax
import jax.numpy as jnp
from jax import lax
from jax.experimental import pallas as pl
from jax.experimental.pallas import tpu as pltpu
from jax.sharding import PartitionSpec as P

HEAD_DIM = 64
masked_score = -1e30
norm_epsilon = 1e-05
low = jnp.bfloat16
full = jnp.float32
STAT_ROWS = 16
KEY_ROWS = 256


def nn(a, b):
    return lax.dot_general(a, b, (((1,), (0,)), ((), ())), preferred_element_type=full)


def nt(a, b):
    return lax.dot_general(a, b, (((1,), (1,)), ((), ())), preferred_element_type=full)


def tn(a, b):
    return lax.dot_general(a, b, (((0,), (0,)), ((), ())), preferred_element_type=full)


def cells(shape, dtype):
    return jax.ShapeDtypeStruct(shape, dtype)


def flops(count):
    return pl.CostEstimate(flops=int(count), bytes_accessed=4_000_000, transcendentals=0)


def kernel_call(body, name, place, operands, outs, scratch=(), anywhere=(), cost=1e9):
    whole = pl.BlockSpec(memory_space=pltpu.VMEM)
    hbm = pl.BlockSpec(memory_space=pl.ANY)
    specs = [pl.BlockSpec(memory_space=pltpu.SMEM)]
    specs += [hbm if n in anywhere else whole for n in range(len(operands))]
    return pl.pallas_call(
        body,
        name=name,
        in_specs=specs,
        out_specs=[whole] * len(outs),
        out_shape=list(outs),
        scratch_shapes=list(scratch),
        cost_estimate=flops(cost),
        compiler_params=pltpu.CompilerParams(vmem_limit_bytes=58 * 2**20),
    )(place, *operands)


def swap(x, axis, mask):
    size = lax.axis_size(axis)
    return lax.ppermute(x, axis, [(i, i ^ mask) for i in range(size)])


def head_exchange(pieces):
    return [pieces[0]] + [swap(pieces[k], "head", k) for k in range(1, 4)]


def seq_gather(x):
    far = swap(x, "seq", 2)
    return [x, swap(x, "seq", 1), far, swap(far, "seq", 1)]


def seq_exchange(pieces):
    return [pieces[0]] + [swap(pieces[j], "seq", j) for j in range(1, 4)]


def gather_parts(part, stages):
    slots = {0: jnp.stack([part] + [swap(part, "head", k) for k in range(1, 4)])}
    for axis, mask, bit in stages:
        for c in list(slots):
            slots[c | bit] = swap(slots[c], axis, mask)
    return [slots[c] for c in range(len(slots))]


def norm_forward(x, gain, shift):
    center = x - jnp.mean(x, axis=-1, keepdims=True)
    spread = jnp.mean(center * center, axis=-1, keepdims=True)
    scale = lax.rsqrt(spread + norm_epsilon)
    normed = center * scale
    return normed * gain + shift, normed, scale


def norm_backward(grad, normed, scale, gain):
    g = grad * gain
    mean_g = jnp.mean(g, axis=-1, keepdims=True)
    mean_gn = jnp.mean(g * normed, axis=-1, keepdims=True)
    return scale * (g - mean_g - normed * mean_gn)


def column_sum(x):
    return jnp.sum(x, axis=0, keepdims=True)


def two_parts(x):
    high = x.astype(low).astype(full)
    return [high, x - high]


def self_project(place, target, weight, bias, query_t, pair_t):
    rows = target.shape[0] // 2
    width = bias.shape[1]
    row = jnp.concatenate([bias[0:1], jnp.zeros((1, width), full), bias[1:2]], axis=1)
    proj = nn(target[...], weight[...]) + row
    lane = lax.broadcasted_iota(jnp.int32, proj.shape, 1)
    proj = jnp.where(lane < width, proj * 0.125, proj)
    turned = proj.T.astype(low)
    for i in range(2):
        part = turned[:, i * rows : (i + 1) * rows]
        query_t[i] = part[:width]
        pair_t[i] = part[width:]


def self_scores(place, key_t, query, j):
    scores = tn(key_t, query)
    seq_place = place[1]
    if j == 0:
        key_pos = lax.broadcasted_iota(jnp.int32, scores.shape, 0)
        query_pos = lax.broadcasted_iota(jnp.int32, scores.shape, 1)
        return jnp.where(query_pos >= key_pos, scores, masked_score)
    return scores + jnp.where((seq_place ^ j) < seq_place, 0.0, masked_score).astype(full)


def self_forward(place, query_t, p0, p1, p2, p3, a0, a1, a2, a3, attn, logs, held):
    pairs = (p0, p1, p2, p3)
    width = query_t.shape[1]
    for i in range(2):
        rows = []
        for h in range(width // HEAD_DIM):
            at = slice(h * HEAD_DIM, (h + 1) * HEAD_DIM)
            vat = slice(width + h * HEAD_DIM, width + (h + 1) * HEAD_DIM)
            query = query_t[i, at]
            scores = [self_scores(place, pairs[j][i, at], query, j) for j in range(4)]
            top = jnp.max(scores[0], axis=0, keepdims=True)
            for j in range(1, 4):
                top = jnp.maximum(top, jnp.max(scores[j], axis=0, keepdims=True))
            total, out = 0.0, 0.0
            for j in range(4):
                weights = jnp.exp(scores[j] - top)
                total = total + jnp.sum(weights, axis=0, keepdims=True)
                out = out + nn(pairs[j][i, vat], weights.astype(low))
            out = out * (1.0 / total)
            attn[i, at] = out
            out = out.astype(low)
            held[2 * i, at] = out[:, :128]
            held[2 * i + 1, at] = out[:, 128:]
            rows.append(top + jnp.log(total))
        rows.append(jnp.zeros((8 - len(rows), rows[0].shape[1]), full))
        logs[i] = jnp.concatenate(rows, axis=0)
    for k, out in enumerate((a0, a1, a2, a3)):
        out[...] = held[k ^ place[0]]


def self_backward(
    place, query_t, p0, p1, p2, p3, attn, logs, g0, g1, g2, g3, dquery, d0, d1, d2, d3, held
):
    pairs = (p0, p1, p2, p3)
    grads = (d0, d1, d2, d3)
    width = query_t.shape[1]
    for k, piece in enumerate((g0, g1, g2, g3)):
        held[k ^ place[0]] = piece[...]
    for i in range(2):
        for h in range(width // HEAD_DIM):
            at = slice(h * HEAD_DIM, (h + 1) * HEAD_DIM)
            vat = slice(width + h * HEAD_DIM, width + (h + 1) * HEAD_DIM)
            query = query_t[i, at]
            grad = jnp.concatenate([held[2 * i, at], held[2 * i + 1, at]], axis=1)
            dot = jnp.sum(grad.astype(full) * attn[i, at], axis=0, keepdims=True)
            log_total = logs[i, h : h + 1]
            dq = 0.0
            for j in range(4):
                key_t, value_t = pairs[j][i, at], pairs[j][i, vat]
                weights = jnp.exp(self_scores(place, key_t, query, j) - log_total)
                dscores = (weights * (tn(value_t, grad) - dot)).astype(low)
                dq = dq + nn(key_t, dscores)
                grads[j][i, at] = nt(query, dscores).astype(low)
                grads[j][i, vat] = nt(grad, weights.astype(low)).astype(low)
            dquery[i, at] = dq.astype(low) * 0.125


def memory_project(place, memory, weight, bias, marks, pair, pair_t, extra):
    item = pl.program_id(0) ^ (place[0] // 2)
    proj = (nn(memory[0], weight[...]) + bias[...]).astype(low)
    heads = weight.shape[1] // 128
    rows = proj.shape[0]
    turned = proj.T
    first = lax.broadcasted_iota(jnp.int32, (STAT_ROWS, rows), 0) == 0
    for h in range(heads):
        pair[0, h] = proj[:, 128 * h : 128 * h + 128]
        pair_t[0, h, 0:128] = turned[128 * h : 128 * h + 128]
        pair_t[0, h, 128 : 128 + STAT_ROWS] = first.astype(full).astype(low)
    live = jnp.where(item == 0, marks[0:1], marks[1:2])
    bias_row = jnp.where(live > 0, 0.0, masked_score)
    column = jnp.broadcast_to(bias_row, (128, rows)).T
    lane = lax.broadcasted_iota(jnp.int32, (rows, 128), 1)
    extra[0] = jnp.where(lane == 0, column, jnp.where(lane < 3, 1.0, 0.0)).astype(low)


def slot_lanes(refs, at):
    return jnp.concatenate([refs[j][a, at] for j in range(4) for a in range(2)], axis=1)


def cross_forward(pair, extra, pair_t, q0, q1, q2, q3, o0, o1, o2, o3):
    queries, outs = (q0, q1, q2, q3), (o0, o1, o2, o3)
    heads, key_count = pair.shape[1], pair.shape[2]
    steps = key_count // KEY_ROWS
    count = 8 * 128
    first = lax.broadcasted_iota(jnp.int32, (STAT_ROWS, count), 0) == 0
    ones_row = first.astype(full).astype(low)
    stats = []
    for h in range(heads):
        query = slot_lanes(queries, slice(64 * h, 64 * h + 64))
        right = jnp.concatenate(
            [query, jnp.zeros((64, count), low), ones_row, jnp.zeros((112, count), low)], axis=0
        )

        def scores_of(n):
            rows = slice(n * KEY_ROWS, (n + 1) * KEY_ROWS)
            return nn(jnp.concatenate([pair[0, h, rows], extra[0, rows]], axis=1), right)

        top = None
        coming = scores_of(0)
        for n in range(steps):
            scores = coming
            if n + 1 < steps:
                coming = scores_of(n + 1)
            here = jnp.max(scores, axis=0, keepdims=True)
            new_top = here if n == 0 else jnp.maximum(top, here)
            weights = jnp.exp(scores - new_top).astype(low)
            part = nn(pair_t[0, h, 64 : 128 + STAT_ROWS, n * KEY_ROWS : (n + 1) * KEY_ROWS], weights)
            total = part if n == 0 else total * jnp.exp(top - new_top) + part
            top = new_top
        amount = total[64:65]
        out = (total[:64] * (1.0 / amount)).astype(low)
        for j in range(4):
            for a in range(2):
                c = (2 * j + a) * 128
                outs[j][a, 64 * h : 64 * h + 64] = out[:, c : c + 128]
        stats += two_parts(top + jnp.log(amount))
    stats.append(jnp.zeros((STAT_ROWS - len(stats), count), full))
    stats = jnp.concatenate(stats, axis=0).astype(low)
    for j in range(4):
        for a in range(2):
            c = (2 * j + a) * 128
            outs[j][a, 64 * heads : 64 * heads + STAT_ROWS] = stats[:, c : c + 128]


def cross_backward(
    place, pair, extra, pair_t, q0, q1, q2, q3, g0, g1, g2, g3, m0, m1, m2, m3, d0, d1, d2, d3,
    held, dquery, score_right, grad_right, query_right, value_right,
):
    queries, grads, douts = (q0, q1, q2, q3), (g0, g1, g2, g3), (d0, d1, d2, d3)
    heads, key_count = pair.shape[1], pair.shape[2]
    count = 8 * 128
    blocks, block_rows = held.shape[0], held.shape[1]
    none = jnp.zeros((64, count), low)
    pad = jnp.zeros((112, count), low)
    one = jnp.ones((1, count), full)
    rest = jnp.zeros((STAT_ROWS - 3, count), full)
    stats = slot_lanes(grads, slice(64 * heads, 64 * heads + STAT_ROWS)).astype(full)
    for h in range(heads):
        at = slice(64 * h, 64 * h + 64)
        query, grad = slot_lanes(queries, at), slot_lanes(grads, at)
        score_rows = jnp.concatenate([one, stats[4 * h : 4 * h + 2], rest], axis=0).astype(low)
        dot_rows = jnp.concatenate([0.0 * one, stats[4 * h + 2 : 4 * h + 4], rest], axis=0).astype(low)
        score_right[...] = jnp.concatenate([query, none, score_rows, pad], axis=0)
        grad_right[...] = jnp.concatenate([none, grad, dot_rows, pad], axis=0)
        query_right[...] = jnp.concatenate([query, none], axis=0)
        value_right[...] = jnp.concatenate([none, grad], axis=0)
        for n in range(key_count // KEY_ROWS):
            rows = slice(n * KEY_ROWS, (n + 1) * KEY_ROWS)
            left = jnp.concatenate([pair[0, h, rows], extra[0, rows]], axis=1)
            weights = jnp.exp(nn(left, score_right[...]))
            dscores = (weights * nn(left, grad_right[...])).astype(low)
            dpair = nt(weights.astype(low), value_right[...]) + nt(dscores, query_right[...])
            dpair = dpair.astype(low)
            done = 0
            while done < KEY_ROWS:
                start = n * KEY_ROWS + done
                block, inner = start // block_rows, start % block_rows
                size = min(KEY_ROWS - done, block_rows - inner)
                held[block, inner : inner + size, 128 * h : 128 * h + 128] = dpair[done : done + size]
                done += size
            part = nn(pair_t[0, h, 0:64, rows], dscores)
            if n == 0:
                dquery[...] = part
            else:
                dquery[...] += part
        for j in range(4):
            for a in range(2):
                c = (2 * j + a) * 128
                douts[j][a, at] = dquery[:, c : c + 128].astype(low)
    for k, out in enumerate((m0, m1, m2, m3)):
        out[0] = held[k ^ place[0]]


def combine_outputs(place, p0, p1, p2, p3, o0, o1, o2, o3):
    parts = (p0, p1, p2, p3)
    width = p0.shape[1] - STAT_ROWS
    heads = width // HEAD_DIM
    for k, out in enumerate((o0, o1, o2, o3)):
        stats = [part[k, width : width + STAT_ROWS].astype(full) for part in parts]
        rows = []
        for h in range(heads):
            at = slice(64 * h, 64 * h + 64)
            logs = [s[2 * h : 2 * h + 1] + s[2 * h + 1 : 2 * h + 2] for s in stats]
            top = jnp.maximum(jnp.maximum(logs[0], logs[1]), jnp.maximum(logs[2], logs[3]))
            shares = [jnp.exp(value - top) for value in logs]
            amount = shares[0] + shares[1] + shares[2] + shares[3]
            inverse = 1.0 / amount
            total = 0.0
            for j in range(4):
                total = total + parts[j][k, at].astype(full) * (shares[j] * inverse)
            out[at] = total.astype(low)
            rows += two_parts(top + jnp.log(amount))
        rows.append(jnp.zeros((STAT_ROWS - len(rows), rows[0].shape[1]), full))
        out[width : width + STAT_ROWS] = jnp.concatenate(rows, axis=0).astype(low)


def combine_queries(place, p0, p1, p2, p3, o0, o1, o2, o3):
    for k, out in enumerate((o0, o1, o2, o3)):
        total = p0[k].astype(full) + p1[k].astype(full) + p2[k].astype(full) + p3[k].astype(full)
        out[...] = total.astype(low) * 0.125


def assemble(slots, scratch, at, part):
    for c, slot in enumerate(slots):
        for k in range(4):
            scratch[k, part ^ c] = slot[k] if at is None else slot[k, at]


def matrix_of(scratch, k):
    parts = scratch[k]
    return parts.reshape(parts.shape[0] * parts.shape[1], parts.shape[2])


def dense_one(
    place, a0, a1, a2, a3, target, s0, s1, s2, s3, query_bias, biases, gains, shifts,
    hidden, hidden_low, normed, scale, q0, q1, q2, q3, out_w, query_w,
):
    part = (place[2] % 2) * 2 + place[1] % 2
    assemble((s0, s1, s2, s3), out_w, 0, part)
    assemble((s0, s1, s2, s3), query_w, 1, part)
    rows = hidden.shape[0]
    total = 0.0
    for k, piece in enumerate((a0, a1, a2, a3)):
        total = total + tn(piece[...], matrix_of(out_w, k))
    mine = target[pl.ds(pl.multiple_of(place[0] * rows, rows), rows), :].astype(full)
    value, n, r = norm_forward(mine + (total + biases[0:1]), gains[0:1], shifts[0:1])
    hidden[...] = value
    value = value.astype(low)
    hidden_low[...] = value
    normed[...] = n
    scale[...] = jnp.broadcast_to(r, scale.shape)
    for k, out in enumerate((q0, q1, q2, q3)):
        query = (nt(value, matrix_of(query_w, k)) + query_bias[k : k + 1]) * 0.125
        out[...] = query.T.astype(low)


def dense_two(place, *refs):
    outs = refs[0:4]
    hidden, cotangent = refs[4:6]
    cross_slots, up_slots, down_slots = refs[6:10], refs[10:18], refs[18:26]
    up_bias, biases, gains, shifts = refs[26:30]
    layer, grad_hidden = refs[30:32]
    grads = refs[32:36]
    shares = refs[36:40]
    rows_out, sums, up_sums = refs[40:43]
    cross_w, up_w, down_w, pre_held, active_held, pre_grad_held, attn_held, sem = refs[43:]
    rows = hidden.shape[0]
    seq_place, data_place = place[1], place[2] % 2
    eighth = data_place * 4 + seq_place
    copies = []
    for c in range(8):
        copies.append(pltpu.make_async_copy(up_slots[c], up_w.at[:, eighth ^ c], sem.at[c]))
        copies.append(pltpu.make_async_copy(down_slots[c], down_w.at[:, eighth ^ c], sem.at[8 + c]))
    for copy in copies:
        copy.start()
    assemble(cross_slots, cross_w, None, data_place * 2 + seq_place % 2)
    width = outs[0].shape[0] - STAT_ROWS
    quarter = width // 4
    total = 0.0
    for k in range(4):
        total = total + tn(outs[k][0:width], matrix_of(cross_w, k))
        for q in range(4):
            attn_held[k, q] = outs[k][q * quarter : (q + 1) * quarter]
    sum_two = hidden[...] + (total + biases[1:2])
    h2, n2, r2 = norm_forward(sum_two, gains[1:2], shifts[1:2])
    h2_low = h2.astype(low)
    for copy in copies:
        copy.wait()
    out = 0.0
    for k in range(4):
        pre = nn(h2_low, matrix_of(up_w, k)) + up_bias[k : k + 1]
        pre_held[k] = pre
        share = 0.5 * (1.0 + lax.erf(pre * 0.7071067811865476))
        active = (pre * share).astype(low)
        out = out + nn(active, matrix_of(down_w, k))
        turned = active.T
        step = turned.shape[0] // 4
        for q in range(4):
            active_held[k, q] = turned[q * step : (q + 1) * step]
    y, n3, r3 = norm_forward(h2 + (out + biases[2:3]), gains[2:3], shifts[2:3])
    layer[...] = y.astype(low)
    cot = cotangent[pl.ds(pl.multiple_of(place[0] * rows, rows), rows), :].astype(full)
    g3 = norm_backward(cot, n3, r3, gains[2:3])
    g3_low = g3.astype(low)
    grad = 0.0
    for k in range(4):
        pre = pre_held[k]
        share = 0.5 * (1.0 + lax.erf(pre * 0.7071067811865476))
        slope = share + pre * (0.3989422804014327 * jnp.exp(-0.5 * pre * pre))
        dpre = (nt(g3_low, matrix_of(down_w, k)) * slope).astype(low)
        grad = grad + nt(dpre, matrix_of(up_w, k))
        up_sums[k : k + 1] = column_sum(dpre.astype(full))
        turned = dpre.T
        step = turned.shape[0] // 4
        for q in range(4):
            pre_grad_held[k, q] = turned[q * step : (q + 1) * step]
    grad = g3 + grad
    g2 = norm_backward(grad, n2, r2, gains[1:2])
    grad_hidden[...] = g2
    g2_low = g2.astype(low)
    for k in range(4):
        dattn = nt(matrix_of(cross_w, k), g2_low).astype(low)
        grads[k][0:width] = dattn
        product = dattn.astype(full) * outs[k][0:width].astype(full)
        stats = outs[k][width : width + STAT_ROWS].astype(full)
        lines = []
        for h in range(width // HEAD_DIM):
            dot = jnp.sum(product[64 * h : 64 * h + 64], axis=0, keepdims=True)
            lines += [-stats[2 * h : 2 * h + 1], -stats[2 * h + 1 : 2 * h + 2]]
            lines += two_parts(-dot)
        lines.append(jnp.zeros((STAT_ROWS - len(lines), rows), full))
        grads[k][width : width + STAT_ROWS] = jnp.concatenate(lines, axis=0).astype(low)
    half = h2_low.shape[1] // 2
    for n, value in enumerate((h2_low, g3_low, g2_low)):
        rows_out[n, 0] = value[:, :half]
        rows_out[n, 1] = value[:, half:]
    step = active_held.shape[2]
    for j in range(4):
        for k in range(4):
            shares[j][k, 0:step] = active_held[k, seq_place ^ j]
            shares[j][k, step : 2 * step] = pre_grad_held[k, seq_place ^ j]
            shares[j][k, 2 * step : 2 * step + quarter] = attn_held[k, seq_place ^ j]
    sums[...] = jnp.concatenate(
        [
            column_sum(g2_low.astype(full)),
            column_sum(g3_low.astype(full)),
            column_sum(grad * n2),
            column_sum(cot * n3),
            column_sum(grad),
            column_sum(cot),
            jnp.zeros((2, h2.shape[1]), full),
        ],
        axis=0,
    )


def dense_three(
    place, d0, d1, d2, d3, a0, a1, a2, a3, grad_hidden, hidden_low, normed, scale,
    s0, s1, s2, s3, gains,
    grad_sum, g0, g1, g2, g3, x0, x1, x2, x3, rows_out, sums, query_sums,
    out_w, query_w, attn_held, query_held,
):
    part = (place[2] % 2) * 2 + place[1] % 2
    assemble((s0, s1, s2, s3), out_w, 0, part)
    assemble((s0, s1, s2, s3), query_w, 1, part)
    total = grad_hidden[...]
    width = d0.shape[0]
    quarter = width // 4
    ones = jnp.ones((8, d0.shape[1]), low)
    for k, (piece, attn) in enumerate(zip((d0, d1, d2, d3), (a0, a1, a2, a3))):
        value = piece[...]
        total = total + tn(value, matrix_of(query_w, k))
        query_sums[8 * k : 8 * k + 8] = nt(ones, value)
        for q in range(4):
            at = slice(q * quarter, (q + 1) * quarter)
            query_held[k, q] = piece[at]
            attn_held[k, q] = attn[at]
    n = normed[...]
    g = norm_backward(total, n, scale[:, 0:1], gains[0:1])
    grad_sum[...] = g
    g_low = g.astype(low)
    for k, out in enumerate((g0, g1, g2, g3)):
        out[...] = nt(matrix_of(out_w, k), g_low).astype(low)
    half = g_low.shape[1] // 2
    for m, value in enumerate((g_low, hidden_low[...])):
        rows_out[m, 0] = value[:, :half]
        rows_out[m, 1] = value[:, half:]
    for j, out in enumerate((x0, x1, x2, x3)):
        for k in range(4):
            out[k, 0:quarter] = attn_held[k, place[1] ^ j]
            out[k, quarter : 2 * quarter] = query_held[k, place[1] ^ j]
    sums[...] = jnp.concatenate(
        [
            column_sum(g_low.astype(full)),
            column_sum(total * n),
            column_sum(total),
            jnp.zeros((5, n.shape[1]), full),
        ],
        axis=0,
    )


def weight_grads(groups):
    def body(place, x0, x1, x2, x3, r0, r1, r2, r3, out):
        shares, rows = (x0, x1, x2, x3), (r0, r1, r2, r3)
        for n, (begin, end) in enumerate(groups):
            for half in range(2):
                right = jnp.concatenate([row[n, half] for row in rows], axis=0)
                for k in range(4):
                    left = jnp.concatenate([share[k, begin:end] for share in shares], axis=1)
                    out[half, k, begin:end] = nn(left, right).astype(low)

    return body


def memory_weight_grad(place, memory, m0, m1, m2, m3, out, sums, total):
    step = pl.program_id(0)
    width = m0.shape[2]
    lines = 0.0
    product = 0.0
    ones = jnp.ones((8, m0.shape[1]), low)
    for k, piece in enumerate((m0, m1, m2, m3)):
        value = piece[0]
        product = product + tn(value, memory[0, k ^ place[0]])
        lines = lines + nn(ones, value)

    @pl.when(step == 0)
    def _():
        total[...] = product
        sums[...] = lines

    @pl.when(step == 1)
    def _():
        sums[...] += lines
        whole = (total[...] + product).astype(low)
        quarter = width // 4
        half = whole.shape[1] // 2
        for q in range(4):
            for n in range(2):
                out[q, n] = whole[q * quarter : (q + 1) * quarter, n * half : (n + 1) * half]


def memory_gradient(place, m0, m1, m2, m3, s0, s1, s2, s3, s4, s5, s6, s7, out, weight):
    eighth = (place[2] % 2) * 4 + place[1]
    assemble((s0, s1, s2, s3, s4, s5, s6, s7), weight, None, eighth)
    for i in range(2):
        total = 0.0
        for k, piece in enumerate((m0, m1, m2, m3)):
            total = total + nn(piece[i], matrix_of(weight, k))
        out[i] = total


def target_partial(place, dquery, dpair, target, weight, o0, o1, o2, o3, grads, sums, held):
    width = dquery.shape[1]
    total = 0.0
    ones = jnp.ones((8, dquery.shape[2]), low)
    lines = 0.0
    for i in range(2):
        turned = jnp.concatenate([dquery[i], dpair[i]], axis=0)
        natural = turned.T
        part = nt(natural, weight[...]).astype(low)
        held[2 * i] = part[:128]
        held[2 * i + 1] = part[128:]
        rows = dquery.shape[2]
        total = total + nn(turned, target[i * rows : (i + 1) * rows])
        lines = lines + nt(ones, turned)
    sums[...] = lines
    total = total.astype(low)
    quarter = total.shape[0] // 4
    half = total.shape[1] // 2
    for q in range(4):
        for n in range(2):
            grads[q, n] = total[q * quarter : (q + 1) * quarter, n * half : (n + 1) * half]
    for k, out in enumerate((o0, o1, o2, o3)):
        out[...] = held[k ^ place[0]]


def add_parts(place, grad, p0, p1, p2, p3, out):
    total = grad[...]
    for part in (p0, p1, p2, p3):
        total = total + part[...].astype(full)
    out[...] = total.astype(low)


def place_rows(place, b0, b1, b2, b3, out):
    rows = b0.shape[0]
    for k, block in enumerate((b0, b1, b2, b3)):
        at = pl.ds(pl.multiple_of((k ^ place[0]) * rows, rows), rows)
        out[at, :] = block[...].astype(full)


def data_total(x):
    size = lax.axis_size("dp")
    place = lax.axis_index("dp")
    if size == 2:
        sent = lax.dynamic_index_in_dim(x, 1 - place, 0, False)
        kept = lax.dynamic_index_in_dim(x, place, 0, False)
        return kept.astype(full) + swap(sent, "dp", 1).astype(full)
    joined = jnp.concatenate([x[0], x[1]], axis=-1).astype(full)
    return lax.psum_scatter(joined, "dp", scatter_dimension=joined.ndim - 1, tiled=True)


def head_total(x, place):
    pieces = head_exchange([x[k] for k in range(4)])
    return sum(piece.astype(full) for piece in pieces)


def ordered(slots, place):
    stacked = jnp.stack(slots)
    return jnp.stack(
        [lax.dynamic_index_in_dim(stacked, q ^ place, 0, False) for q in range(4)]
    )


def seq_reduce_own(grads, seq_place):
    pieces = [
        lax.dynamic_index_in_dim(grads, seq_place ^ j, 0, False) for j in range(4)
    ]
    received = seq_exchange(pieces)
    return sum(piece.astype(full) for piece in received).astype(low)


def shards(
    target, memory, memory_mark, self_in, self_in_bias, self_out, cross_in, cross_in_bias,
    cross_out, ffn_up, ffn_up_bias, ffn_down, out_biases, norm_gains, norm_biases, cotangent,
):
    items, rows, model = target.shape
    width = self_in.shape[2]
    heads = width // HEAD_DIM
    hidden_units = ffn_up.shape[1]
    memory_rows = memory.shape[1]
    tokens = items * rows
    block = tokens // 4
    head_place = lax.axis_index("head")
    seq_place = lax.axis_index("seq")
    data_place = lax.axis_index("dp")
    place = jnp.stack([head_place, seq_place, data_place]).astype(jnp.int32)
    near = (data_place % 2) * 2 + seq_place % 2
    eighth = (data_place % 2) * 4 + seq_place
    flat_target = target.reshape(tokens, model)
    flat_cotangent = cotangent.reshape(tokens, model)

    self_weight = self_in.reshape(model, 3 * width)
    query_t, pair_t = kernel_call(
        self_project, "self_project", place, (flat_target, self_weight, self_in_bias),
        (cells((items, width, rows), low), cells((items, 2 * width, rows), low)),
    )
    pairs = seq_gather(pair_t)

    cross_query_t = cross_in[:, 0].T
    early = jnp.stack([self_out, cross_query_t])
    quarter = width // 4
    early = lax.dynamic_slice_in_dim(early, near * quarter, quarter, 1)
    near_stages = (("dp", 1, 2), ("seq", 1, 1))
    early_slots = gather_parts(early, near_stages)
    bias_row = jnp.concatenate(
        [ffn_up_bias, cross_in_bias[0], jnp.zeros((256 - width,), full)]
    ).reshape(8, -1)
    bias_rows = jnp.stack([bias_row] + [swap(bias_row, "head", k) for k in range(1, 4)])
    bias_rows = bias_rows.reshape(4, -1)
    up_bias, query_bias = bias_rows[:, :hidden_units], bias_rows[:, hidden_units : hidden_units + width]
    cross_slots = gather_parts(
        lax.dynamic_slice_in_dim(cross_out, near * quarter, quarter, 0), near_stages
    )
    step = model // 8
    up_slots = gather_parts(
        lax.dynamic_slice_in_dim(ffn_up, eighth * step, step, 0),
        (("dp", 1, 4), ("seq", 2, 2), ("seq", 1, 1)),
    )
    step = hidden_units // 8
    down_slots = gather_parts(
        lax.dynamic_slice_in_dim(ffn_down, eighth * step, step, 0),
        (("seq", 2, 2), ("dp", 1, 4), ("seq", 1, 1)),
    )

    pair_weight = cross_in[:, 1:].reshape(model, 2, heads, HEAD_DIM)
    pair_weight = jnp.transpose(pair_weight, (0, 2, 1, 3)).reshape(model, 2 * width)
    value_bias = cross_in_bias[1].reshape(heads, 1, HEAD_DIM)
    pair_bias = jnp.concatenate([jnp.zeros_like(value_bias), value_bias], axis=1).reshape(1, 2 * width)
    step = 2 * width // 8
    pair_slots = gather_parts(
        lax.dynamic_slice_in_dim(pair_weight.T, eighth * step, step, 0),
        (("dp", 1, 4), ("seq", 2, 2), ("seq", 1, 1)),
    )
    row_step = 512
    row_steps = memory_rows // row_step
    memory_pair, memory_pair_t, memory_extra = pl.pallas_call(
        memory_project,
        name="memory_project",
        grid_spec=pltpu.PrefetchScalarGridSpec(
            num_scalar_prefetch=1,
            grid=(items, row_steps),
            in_specs=[
                pl.BlockSpec((1, row_step, model), lambda i, r, p: (i ^ (p[0] // 2), r, 0)),
                pl.BlockSpec((model, 2 * width), lambda i, r, p: (0, 0)),
                pl.BlockSpec((1, 2 * width), lambda i, r, p: (0, 0)),
                pl.BlockSpec((items, row_step), lambda i, r, p: (0, p[1] * row_steps + r)),
            ],
            out_specs=[
                pl.BlockSpec((1, heads, row_step, 128), lambda i, r, p: (i, 0, r, 0)),
                pl.BlockSpec((1, heads, 128 + STAT_ROWS, row_step), lambda i, r, p: (i, 0, 0, r)),
                pl.BlockSpec((1, row_step, 128), lambda i, r, p: (i, r, 0)),
            ],
        ),
        out_shape=[
            cells((items, heads, memory_rows, 128), low),
            cells((items, heads, 128 + STAT_ROWS, memory_rows), low),
            cells((items, memory_rows, 128), low),
        ],
        cost_estimate=flops(4e9),
        compiler_params=pltpu.CompilerParams(vmem_limit_bytes=58 * 2**20),
    )(place, memory, pair_weight, pair_bias, memory_mark)

    piece = cells((width, block), low)
    attn_pieces = kernel_call(
        self_forward, "self_forward", place, (query_t, *pairs),
        [piece] * 4 + [cells((items, width, rows), full), cells((items, 8, rows), full)],
        scratch=[pltpu.VMEM((4, width, block), low)],
    )
    attn_one, logs_one = attn_pieces[4:]
    attn_pieces = head_exchange(attn_pieces[:4])

    near_matrix = pltpu.VMEM((4, 4, quarter, model), low)
    token_rows, token_rows_low = cells((block, model), full), cells((block, model), low)
    hidden_one, hidden_one_low, normed_one, scale_one, *queries = kernel_call(
        dense_one, "dense_one", place,
        (*attn_pieces, flat_target, *early_slots, query_bias, out_biases, norm_gains, norm_biases),
        [token_rows, token_rows_low, token_rows, cells((block, 128), full)] + [piece] * 4,
        scratch=[near_matrix, near_matrix],
    )
    queries = seq_gather(jnp.stack(head_exchange(queries)))

    pair_specs = [
        pl.BlockSpec((1, heads, memory_rows, 128), lambda i, *p: (i, 0, 0, 0)),
        pl.BlockSpec((1, memory_rows, 128), lambda i, *p: (i, 0, 0)),
        pl.BlockSpec((1, heads, 128 + STAT_ROWS, memory_rows), lambda i, *p: (i, 0, 0, 0)),
    ]
    slot = pl.BlockSpec((2, width, block), lambda i, *p: (i, 0, 0))
    stat_slot = pl.BlockSpec((2, width + STAT_ROWS, block), lambda i, *p: (i, 0, 0))
    outs = pl.pallas_call(
        cross_forward,
        name="cross_forward",
        grid=(items,),
        in_specs=pair_specs + [slot] * 4,
        out_specs=[stat_slot] * 4,
        out_shape=[cells((4, width + STAT_ROWS, block), low)] * 4,
        cost_estimate=flops(15e9),
        compiler_params=pltpu.CompilerParams(vmem_limit_bytes=58 * 2**20),
    )(memory_pair, memory_extra, memory_pair_t, *queries)
    stat_piece = cells((width + STAT_ROWS, block), low)
    outs = kernel_call(
        combine_outputs, "combine_outputs", place, seq_exchange(outs), [stat_piece] * 4
    )
    outs = head_exchange(outs)

    share_rows = 2 * (hidden_units // 4) + quarter
    half = model // 2
    dense = kernel_call(
        dense_two, "dense_two", place,
        (*outs, hidden_one, flat_cotangent, *cross_slots, *up_slots, *down_slots,
         up_bias, out_biases, norm_gains, norm_biases),
        [token_rows_low, token_rows] + [stat_piece] * 4
        + [cells((4, share_rows, block), low)] * 4
        + [cells((3, 2, block, half), low), cells((8, model), full), cells((4, hidden_units), full)],
        scratch=[
            near_matrix,
            pltpu.VMEM((4, 8, model // 8, hidden_units), low),
            pltpu.VMEM((4, 8, hidden_units // 8, model), low),
            pltpu.VMEM((4, block, hidden_units), full),
            pltpu.VMEM((4, 4, hidden_units // 4, block), low),
            pltpu.VMEM((4, 4, hidden_units // 4, block), low),
            pltpu.VMEM((4, 4, quarter, block), low),
            pltpu.SemaphoreType.DMA((16,)),
        ],
        anywhere=range(10, 26),
        cost=3e9,
    )
    layer_block, grad_hidden = dense[0:2]
    grads = seq_gather(jnp.stack(head_exchange(dense[2:6])))
    shares, row_pack, sums_mid, up_sums = dense[6:10], dense[10], dense[11], dense[12]

    memory_block = memory_rows // 4
    back = pl.pallas_call(
        cross_backward,
        name="cross_backward",
        grid_spec=pltpu.PrefetchScalarGridSpec(
            num_scalar_prefetch=1,
            grid=(items,),
            in_specs=pair_specs + [slot] * 4 + [stat_slot] * 4,
            out_specs=[
                pl.BlockSpec((1, memory_block, 2 * width), lambda i, p: (i ^ (p[0] // 2), 0, 0))
            ] * 4 + [slot] * 4,
            scratch_shapes=[
                pltpu.VMEM((4, memory_block, 2 * width), low),
                pltpu.VMEM((64, 1024), full),
                pltpu.VMEM((256, 1024), low),
                pltpu.VMEM((256, 1024), low),
                pltpu.VMEM((128, 1024), low),
                pltpu.VMEM((128, 1024), low),
            ],
        ),
        out_shape=[cells((items, memory_block, 2 * width), low)] * 4
        + [cells((4, width, block), low)] * 4,
        cost_estimate=flops(30e9),
        compiler_params=pltpu.CompilerParams(vmem_limit_bytes=58 * 2**20),
    )(place, memory_pair, memory_extra, memory_pair_t, *queries, *grads)
    memory_pieces, dqueries = back[:4], back[4:]
    dqueries = kernel_call(
        combine_queries, "combine_queries", place, seq_exchange(dqueries), [piece] * 4
    )
    dqueries = head_exchange(dqueries)

    late = kernel_call(
        dense_three, "dense_three", place,
        (*dqueries, *attn_pieces, grad_hidden, hidden_one_low, normed_one, scale_one,
         *early_slots, norm_gains),
        [token_rows] + [piece] * 4 + [cells((4, 2 * quarter, block), low)] * 4
        + [cells((2, 2, block, half), low), cells((8, model), full), cells((32, width), full)],
        scratch=[near_matrix, near_matrix]
        + [pltpu.VMEM((4, 4, quarter, block), low)] * 2,
    )
    grad_sum_one = late[0]
    grads_one = head_exchange(late[1:5])
    shares_late, row_pack_late, sums_late, query_sums = late[5:9], late[9], late[10], late[11]

    pair_cells = cells((items, 2 * width, rows), low)
    dquery, *dpairs = kernel_call(
        self_backward, "self_backward", place,
        (query_t, *pairs, attn_one, logs_one, *grads_one),
        [cells((items, width, rows), low)] + [pair_cells] * 4,
        scratch=[pltpu.VMEM((4, width, block), low)],
    )
    kept = dpairs[0].astype(full) + swap(dpairs[1], "seq", 1).astype(full)
    sent = dpairs[2].astype(full) + swap(dpairs[3], "seq", 1).astype(full)
    dpair = (kept + swap(sent.astype(low), "seq", 2).astype(full)).astype(low)

    last = kernel_call(
        target_partial, "target_partial", place, (dquery, dpair, flat_target, self_weight),
        [token_rows_low] * 4
        + [cells((4, 2, 3 * width // 4, half), low), cells((8, 3 * width), full)],
        scratch=[pltpu.VMEM((4, block, model), low)],
    )
    target_block = kernel_call(
        add_parts, "add_parts", place, (grad_sum_one, *head_exchange(last[:4])), [token_rows_low]
    )[0]

    def all_rows(part, name):
        blocks = [part] + [swap(part, "head", k) for k in range(1, 4)]
        out = kernel_call(place_rows, name, place, blocks, [cells((tokens, model), full)])[0]
        return out.reshape(items, rows, model)

    layer_out = all_rows(layer_block, "layer_rows")
    target_grad = all_rows(target_block, "target_rows")

    received = head_exchange(memory_pieces)
    memory_grad = kernel_call(
        memory_gradient, "memory_gradient", place, (*received, *pair_slots),
        [cells((items, memory_block, model), full)],
        scratch=[pltpu.VMEM((4, 8, 2 * width // 8, model), low)],
    )[0]

    def token_weights(shares, pack, groups, name):
        parts = kernel_call(
            weight_grads(groups), name, place, (*seq_exchange(shares), *seq_gather(pack)),
            [cells((2, 4, groups[-1][1], half), low)],
        )[0]
        mine = head_total(data_total(parts).astype(low), head_place).astype(low)
        return ordered(seq_gather(mine), seq_place)

    unit_step = hidden_units // 4
    mid = token_weights(
        shares, row_pack,
        ((unit_step, 2 * unit_step), (0, unit_step), (2 * unit_step, share_rows)), "weights_mid",
    )
    ffn_down_grad = mid[:, 0:unit_step].reshape(hidden_units, -1).astype(full)
    ffn_up_grad = mid[:, unit_step : 2 * unit_step].reshape(hidden_units, -1).T.astype(full)
    cross_out_grad = mid[:, 2 * unit_step :].reshape(width, -1).astype(full)
    end = token_weights(
        shares_late, row_pack_late, ((0, quarter), (quarter, 2 * quarter)), "weights_late"
    )
    self_out_grad = end[:, 0:quarter].reshape(width, -1).astype(full)
    cross_query_grad = end[:, quarter:].reshape(width, -1)

    memory_parts, memory_sums = pl.pallas_call(
        memory_weight_grad,
        name="memory_weight_grad",
        grid_spec=pltpu.PrefetchScalarGridSpec(
            num_scalar_prefetch=1,
            grid=(items,),
            in_specs=[pl.BlockSpec((1, 4, memory_block, model), lambda i, p: (i, 0, 0, 0))]
            + [pl.BlockSpec((1, memory_block, 2 * width), lambda i, p: (i, 0, 0))] * 4,
            out_specs=[
                pl.BlockSpec((4, 2, width // 2, half), lambda i, p: (0, 0, 0, 0)),
                pl.BlockSpec((8, 2 * width), lambda i, p: (0, 0)),
            ],
            scratch_shapes=[pltpu.VMEM((2 * width, model), full)],
        ),
        out_shape=[cells((4, 2, width // 2, half), low), cells((8, 2 * width), full)],
        cost_estimate=flops(2e9),
        compiler_params=pltpu.CompilerParams(vmem_limit_bytes=58 * 2**20),
    )(place, memory.reshape(items, 4, memory_block, model), *memory_pieces)

    def own_weights(grads):
        mine = data_total(seq_reduce_own(grads, seq_place)).astype(low)
        whole = ordered(seq_gather(mine), seq_place)
        return whole.reshape(-1, whole.shape[2])

    self_in_grad = own_weights(last[4])
    share = self_in_grad.shape[1]
    self_in_grad = self_in_grad.T.reshape(share, 3, width).astype(full)
    pair_grad = own_weights(memory_parts).T.reshape(share, heads, 2, HEAD_DIM)
    pair_grad = jnp.transpose(pair_grad, (0, 2, 1, 3)).reshape(share, 2, width)
    cross_in_grad = jnp.concatenate([cross_query_grad.T[:, None], pair_grad], axis=1).astype(full)

    up_own = up_sums
    query_own = query_sums.reshape(4, 8, width)[:, 0]
    by_head = jnp.concatenate([up_own, query_own], axis=1)
    by_head = jnp.stack(
        [lax.dynamic_index_in_dim(by_head, t ^ head_place, 0, False) for t in range(4)]
    )
    value_sums = memory_sums[0].reshape(heads, 2, HEAD_DIM)[:, 1].reshape(width)
    own_sums = jnp.concatenate([last[5][0, :width], last[5][0, 2 * width :], value_sums])
    sums_all, by_head = lax.psum(
        (jnp.concatenate([sums_late[0:3], sums_mid[0:6]]), by_head), ("dp", "seq", "head")
    )
    own_sums = lax.psum(own_sums, ("dp", "seq"))
    mine = lax.dynamic_index_in_dim(by_head, head_place, 0, False)
    self_bias_grad = own_sums[: 2 * width].reshape(2, width)
    cross_bias_grad = jnp.stack([mine[hidden_units:], own_sums[2 * width :]])
    out_bias_grad = jnp.stack([sums_all[0], sums_all[3], sums_all[4]])
    gain_grad = jnp.stack([sums_all[1], sums_all[5], sums_all[6]])
    shift_grad = jnp.stack([sums_all[2], sums_all[7], sums_all[8]])
    return (
        layer_out,
        target_grad,
        memory_grad,
        self_in_grad,
        self_bias_grad,
        self_out_grad,
        cross_in_grad,
        cross_bias_grad,
        cross_out_grad,
        ffn_up_grad,
        mine[:hidden_units],
        ffn_down_grad,
        out_bias_grad,
        gain_grad,
        shift_grad,
    )


def solution(mesh):
    return jax.shard_map(
        shards,
        mesh=mesh,
        in_specs=(
            P("dp", "seq", None),
            P("dp", "seq", None),
            P("dp", None),
            P(None, None, "head"),
            P(None, "head"),
            P("head", None),
            P(None, None, "head"),
            P(None, "head"),
            P("head", None),
            P(None, "head"),
            P("head"),
            P("head", None),
            P(),
            P(),
            P(),
            P("dp", "seq", None),
        ),
        out_specs=(
            P("dp", "seq", None),
            P("dp", "seq", None),
            P("dp", ("seq", "head"), None),
            P("dp", None, "head"),
            P(None, "head"),
            P("head", "dp"),
            P("dp", None, "head"),
            P(None, "head"),
            P("head", "dp"),
            P("dp", "head"),
            P("head"),
            P("head", "dp"),
            P(),
            P(),
            P(),
        ),
        check_vma=False,
    )
```

time: 1700 us -> 619 us (0.36)
  waiting for transfers between devices: 1030 us -> 209 us
  local copies, waits for them, and re-layouts: 269 us -> 30.9 us
  matrix products: 170 us -> 0 us
  starting transfers between devices: 1.47 us -> 152 us
  Pallas kernels: 0 us -> 141 us
  loops' own time: 84.8 us -> 0 us
  other arithmetic: 93.2 us -> 19.2 us
  blocking collectives: 23.4 us -> 56.8 us
    reduce_scatter x9 -> x0, waiting for transfers between devices: 487 us -> none  [the longest x1 164 us: shards(): lax.psum_scatter(memory_part, 'head', scatter_dimension=1, tiled=True)]
    psum x7 -> x0, waiting for transfers between devices: 465 us -> none  [the longest x3 197 us: head_grad_total(): return lax.psum(matrix, 'head')]
    ppermute x0 -> x133, waiting for transfers between devices: none -> 209 us  [swap(): return lax.ppermute(x, axis, [(i, i ^ mask) for i in range(size)])]
    dot_general x119 -> x0, matrix products: 170 us -> none  [the longest x14 42.4 us: second_pass(): jnp.einsum('bhqk,bkhe->bqhe', weights, value_heads, preferred_element_typ...]
    ppermute x0 -> x133, starting transfers between devices: none -> 152 us  [swap(): return lax.ppermute(x, axis, [(i, i ^ mask) for i in range(size)])]
    pallas_call x0 -> x19, Pallas kernels: none -> 141 us  [the longest x15 70.6 us: kernel_call(): pl.pallas_call(body, name=name, in_specs=specs, out_specs=[whole] * len(o...]
    dynamic_update_slice x14 -> x0, local copies, waits for them, and re-layouts: 113 us -> none  [block_step(): lax.dynamic_update_slice_in_dim(grad_pair, block_grad, offset, 1)]
    another operation x6 -> x0, loops' own time: 84.8 us -> none  [the longest x2 29.5 us: attend_backward(): (grad_queries, grad_pair), _ = lax.scan(block_step, initial, offsets)]
  transfers between devices with their start and end apart: 18 -> 133, of which waited for: 18 -> 39; matrix products, arithmetic and copies ran while one was open for 3% -> 6% of each run, Pallas kernels for 0% -> 22%
where the time goes in v1:
time: 619 us; the launch traced here: 611 us
  waiting for transfers between devices  209 us (34%)
  starting transfers between devices  152 us (25%)
  Pallas kernels  141 us (23%)
  blocking collectives  56.8 us (9%)
  local copies, waits for them, and re-layouts  30.9 us (5%)
  other arithmetic  19.2 us (3%)
    ppermute x133, waiting for transfers between devices, swap(): return lax.ppermute(x, axis, [(i, i ^ mask) for i in range(size)])  209 us
    ppermute x133, starting transfers between devices, swap(): return lax.ppermute(x, axis, [(i, i ^ mask) for i in range(size)])  152 us
    pallas_call x15, Pallas kernels, kernel_call(): pl.pallas_call(body, name=name, in_specs=specs, out_specs=[whole] * len(o...  70.6 us
    psum x1, blocking collectives, shards(): lax.psum((jnp.concatenate([sums_late[0:3], sums_mid[0:6]]), by_head), ('d...  43.1 us
    pallas_call x1, Pallas kernels, shards(): pl.pallas_call(cross_backward, name='cross_backward', grid_spec=pltpu.Pre...  39 us
    pallas_call x1, Pallas kernels, shards(): pl.pallas_call(cross_forward, name='cross_forward', grid=(items,), in_spe...  15.5 us
    psum x1, blocking collectives, shards(): own_sums = lax.psum(own_sums, ('dp', 'seq'))  13.6 us
  transfers between devices with their start and end apart: 133, of which 39 were waited for; matrix products, arithmetic and copies ran while one was open for 6% of the time, Pallas kernels for 22%

profile of v1, /device:TPU:9, one launch (start us, length us, event | category | flops | bytes accessed | tf_op | source)
XLA Modules:
  0.0 610.6 jit_solution(11010139809651290073)
XLA Ops:
  7.4 3.2 self_project.1
  12.4 5.6 collective-permute-done.8
  19.6 2.7 collective-permute-start.13
  27.8 4.5 collective-permute-start
  38.3 5.3 collective-permute-done.34
  45.0 4.1 collective-permute-start.43
  49.9 5.5 self_forward.1
  62.7 6.9 %collective-permute-done.5.a3 = bf16[192,128]{1,0:T(8,128)(2,1)S(1)} collective-permute-done((bf16[192,128]{1,0:T(8,128)(2,1)}, bf16[192,128]{1,0:T(8,128)(2,1)S(1)}, u32[]{:S(2)}, u32[]{:S(2)}) %collective-permute-start.5) | collective-permute-done | bytes 49184 | tf_op jit(solution)/shard_map/ppermute | solution.py:56
  73.2 3.9 dense_one.1
  94.6 16.1 %collective-permute-done.19.q2 = bf16[4,192,128]{2,1,0:T(8,128)(2,1)} collective-permute-done((bf16[4,192,128]{2,1,0:T(8,128)(2,1)}, bf16[4,192,128]{2,1,0:T(8,128)(2,1)}, u32[]{:S(2)}, u32[]{:S(2)}) %collective-permute-start.19) | collective-permute-done | bytes 196640 | tf_op jit(solution)/shard_map/ppermute | solution.py:56
  110.7 2.6 collective-permute-start.20
  113.3 8.9 %memory_project.1 = (bf16[2,3,1536,128]{3,2,1,0:T(8,128)(2,1)}, bf16[2,3,144,1536]{3,2,1,0:T(8,128)(2,1)}, bf16[2,1536,128]{2,1,0:T(8,128)(2,1)}) custom-call(s32[3]{0:T(128)} %pad_add_fusion.place, bf16[2,1536,768]{2,1,0:T(8,128)(2,1)} %memory.1, bf16[768,384]{1,0:T(8,128)(2,1)} %copy.40.weight, f32[1,384]{1,0:T(1,128)} %reshape.134.bias, s32[2,6144]{1,0:T(2,128)} %marks.1), custom_call_target="tpu_custom_call" | custom-call | flops 4000000000 | bytes 4000000 | tf_op jit(solution)/shard_map/memory_project/pallas_call | solution.py:694
  125.0 15.5 %cross_forward.1 = (bf16[4,208,128]{2,1,0:T(8,128)(2,1)}, bf16[4,208,128]{2,1,0:T(8,128)(2,1)}, bf16[4,208,128]{2,1,0:T(8,128)(2,1)}, bf16[4,208,128]{2,1,0:T(8,128)(2,1)}) custom-call(bf16[2,3,1536,128]{3,2,1,0:T(8,128)(2,1)} %get-tuple-element.92.pair, bf16[2,1536,128]{2,1,0:T(8,128)(2,1)} %get-tuple-element.93.extra, ...), custom_call_target="tpu_custom_call" | custom-call | flops 15000000512 | bytes 4000000 | tf_op jit(solution)/shard_map/cross_forward/pallas_call | solution.py:747
  144.0 4.3 collective-permute-done.22.p2
  149.7 3.4 collective-permute-done.23.p3
  164.7 13.1 %dense_two.1 = (bf16[128,768]{1,0:T(8,128)(2,1)}, f32[128,768]{1,0:T(8,128)}, bf16[208,128]{1,0:T(8,128)(2,1)}, bf16[208,128]{1,0:T(8,128)(2,1)}, bf16[208,128]{...) custom-call(s32[3]{0:T(128)} %pad_add_fusion.place, ...), custom_call_target="tpu_custom_call" | custom-call | flops 3000000000 | bytes 4000000 | tf_op jit(solution)/shard_map/dense_two/pallas_call | solution.py:42
  185.4 2.8 collective-permute-start.53
  189.3 4.5 collective-permute-start.59
  195.9 9.8 %collective-permute-done.55.b3 = bf16[128,768]{1,0:T(8,128)(2,1)S(1)} collective-permute-done((bf16[128,768]{1,0:T(8,128)(2,1)}, bf16[128,768]{1,0:T(8,128)(2,1)S(1)}, u32[]{:S(2)}, u32[]{:S(2)}) %collective-permute-start.55) | collective-permute-done | bytes 196640 | tf_op jit(solution)/shard_map/ppermute | solution.py:56
  206.5 2.5 layer_rows.1
  210.3 39.0 %cross_backward.1 = (bf16[2,384,384]{2,1,0:T(8,128)(2,1)}, bf16[2,384,384]{2,1,0:T(8,128)(2,1)}, bf16[2,384,384]{2,1,0:T(8,128)(2,1)}, bf16[2,384,384]{2,1,0:T(8...) custom-call(s32[3]{0:T(128)} %pad_add_fusion.place, ...), custom_call_target="tpu_custom_call" | custom-call | flops 30000001024 | bytes 4000000 | tf_op jit(solution)/shard_map/cross_backward/pallas_call | solution.py:790
  249.4 6.9 %memory_weight_grad.1 = (bf16[4,2,96,384]{3,2,1,0:T(8,128)(2,1)}, f32[8,384]{1,0:T(8,128)}) custom-call(s32[3]{0:T(128)} %pad_add_fusion.place, bf16[2,4,384,768]{3,2,1,0:T(8,128)(2,1)} %bitcast.245, bf16[2,384,384]{2,1,0:T(8,128)(2,1)} %get-tuple-element.147.m0, bf16[2,384,384]{2,1,0:T(8,128)(2,1)} %get-tuple-element.148.m1, ...), custom_call_target="tpu_custom_call" | custom-call | flops 2000000000 | bytes 4000000 | tf_op jit(solution)/shard_map/memory_weight_grad/pallas_call | solution.py:891
  262.6 2.6 collective-permute-done.114
  266.4 2.5 collective-permute-done.115
  274.3 2.6 collective-permute-done.64.p3
  289.1 4.3 dense_three.1
  296.9 43.1 %all-reduce.1 = (f32[4,960]{1,0:T(4,128)}, f32[9,768]{1,0:T(8,128)}) all-reduce(f32[4,960]{1,0:T(4,128)S(1)} %pad_maximum_fusion.20, f32[9,768]{1,0:T(8,128)S(1)} %pad_maximum_fusion.19), channel_id=1, replica_groups=mesh['dp'=2,'seq'=4,'head'=4] {'dp','seq','head'}, use_global_device_ids=true, to_apply=%region_1.2 | all-reduce | flops 10752 | bytes 86016 | tf_op jit(solution)/shard_map/psum | solution.py:930
  341.0 2.8 collective-permute-start.123
  347.5 17.1 %collective-permute-done.122.x3 = bf16[4,432,128]{2,1,0:T(8,128)(2,1)S(1)} collective-permute-done((bf16[4,432,128]{2,1,0:T(8,128)(2,1)}, bf16[4,432,128]{2,1,0:T(8,128)(2,1)S(1)}, u32[]{:S(2)}, u32[]{:S(2)}) %collective-permute-start.122) | collective-permute-done | bytes 442400 | tf_op jit(solution)/shard_map/ppermute | solution.py:56
  373.0 9.2 %self_backward.1 = (bf16[2,192,256]{2,1,0:T(8,128)(2,1)}, bf16[2,384,256]{2,1,0:T(8,128)(2,1)}, bf16[2,384,256]{2,1,0:T(8,128)(2,1)}, bf16[2,384,256]{2,1,0:T(8,128)(2,1)}, bf16[2,384,256]{2,1,0:T(8,128)(2,1)}) custom-call(s32[3]{0:T(128)} %pad_add_fusion.place, bf16[2,192,256]{2,1,0:T(8,128)(2,1)} %get-tuple-element.95.query_t, ...), custom_call_target="tpu_custom_call" | custom-call | flops 1000000000 | bytes 4000000 | tf_op jit(solution)/shard_map/self_backward/pallas_call | solution.py:42
  389.6 3.3 collective-permute-done.104.r2
  394.3 32.4 %collective-permute-done.81.m2 = bf16[2,384,384]{2,1,0:T(8,128)(2,1)S(1)} collective-permute-done((bf16[2,384,384]{2,1,0:T(8,128)(2,1)}, bf16[2,384,384]{2,1,0:T(8,128)(2,1)S(1)}, u32[]{:S(2)}, u32[]{:S(2)}) %collective-permute-start.81) | collective-permute-done | bytes 589856 | tf_op jit(solution)/shard_map/ppermute | solution.py:56
  426.8 13.1 %collective-permute-done.82.m3 = bf16[2,384,384]{2,1,0:T(8,128)(2,1)S(1)} collective-permute-done((bf16[2,384,384]{2,1,0:T(8,128)(2,1)}, bf16[2,384,384]{2,1,0:T(8,128)(2,1)S(1)}, u32[]{:S(2)}, u32[]{:S(2)}) %collective-permute-start.82) | collective-permute-done | bytes 589856 | tf_op jit(solution)/shard_map/ppermute | solution.py:56
  441.7 6.5 %memory_gradient.1 = f32[2,384,768]{2,1,0:T(8,128)} custom-call(s32[3]{0:T(128)} %pad_add_fusion.place, bf16[2,384,384]{2,1,0:T(8,128)(2,1)} %get-tuple-element.147.m0, bf16[2,384,384]{2,1,0:T(8,128)(2,1)} %copy-done.13, bf16[2,384,384]{2,1,0:T(8,128)(2,1)} %copy-done.20, bf16[2,384,384]{2,1,0:T(8,128)(2,1)} %copy-done.21, bf16[4,48,768]{2,1,0:T(8,128)(2,1)} %copy-done.6, ...), custom_call_target="tpu_custom_call" | custom-call | flops 1000000000 | bytes 4000000 | tf_op jit(solution)/shard_map/memory_gradient/pallas_call | solution.py:42
  448.2 5.9 weights_mid.1
  459.7 3.8 weights_late.1
  464.4 4.0 target_partial.1
  477.0 13.6 %psum.21 = f32[576]{0:T(1024)S(1)} all-reduce(f32[576]{0:T(1024)S(1)} %pad_maximum_fusion.29), channel_id=1, replica_groups=mesh['dp'=2,'seq'=4,'head'=4] {'dp','seq'}, use_global_device_ids=true, to_apply=%region_0.1 | all-reduce | flops 576 | bytes 4608 | tf_op jit(solution)/shard_map/psum | solution.py:933
  491.0 2.8 collective-permute-done.76.p3
  498.5 27.6 %collective-permute-done.106 = bf16[4,96,384]{2,1,0:T(8,128)(2,1)S(1)} collective-permute-done((bf16[4,96,384]{2,1,0:T(8,128)(2,1)}, bf16[4,96,384]{2,1,0:T(8,128)(2,1)S(1)}, u32[]{:S(2)}, u32[]{:S(2)}) %collective-permute-start.106) | collective-permute-done | bytes 294944 | tf_op jit(solution)/shard_map/ppermute | solution.py:56
  530.3 2.6 collective-permute-start.78
  534.1 3.5 collective-permute-done.96
  537.6 10.9 %collective-permute-start.111 = (bf16[96,384]{1,0:T(8,128)(2,1)S(1)}, bf16[96,384]{1,0:T(8,128)(2,1)S(1)}, u32[]{:S(2)}, u32[]{:S(2)}) collective-permute-start(bf16[96,384]{1,0:T(8,128)(2,1)S(1)} %fusion.16), channel_id=1, source_target_pairs={{0,8},{4,12},{8,0},{12,4},{1,9},{5,13},{9,1},{13,5},{2,10},{6,14},... | collective-permute-start | bytes 221192 | tf_op jit(solution)/shard_map/ppermute | solution.py:56
  553.3 5.4 collective-permute-start.110
  559.2 2.6 target_rows.1
  566.9 10.8 %collective-permute-done.127 = bf16[432,384]{1,0:T(8,128)(2,1)S(1)} collective-permute-done((bf16[432,384]{1,0:T(8,128)(2,1)S(1)}, bf16[432,384]{1,0:T(8,128)(2,1)S(1)}, u32[]{:S(2)}, u32[]{:S(2)}) %collective-permute-start.127) | collective-permute-done | bytes 331808 | tf_op jit(solution)/shard_map/ppermute | solution.py:56
  579.9 14.8 %collective-permute-done.129 = bf16[432,384]{1,0:T(8,128)(2,1)S(1)} collective-permute-done((bf16[432,384]{1,0:T(8,128)(2,1)S(1)}, bf16[432,384]{1,0:T(8,128)(2,1)S(1)}, u32[]{:S(2)}, u32[]{:S(2)}) %collective-permute-start.129) | collective-permute-done | bytes 331808 | tf_op jit(solution)/shard_map/ppermute | solution.py:56
  598.0 4.8 collective-permute-done.131
  (527 shorter events, 184.8 us)
Async XLA Ops:
  10.6 23.1 %collective-permute-start.1 = (bf16[2,384,256]{2,1,0:T(8,128)(2,1)}, bf16[2,384,256]{2,1,0:T(8,128)(2,1)}, u32[]{:S(2)}, u32[]{:S(2)}) collective-permute-start(bf16[2,384,256]{2,1,0:T(8,128)(2,1)} %get-tuple-element.96.p0), channel_id=1, source_target_pairs={{0,8},{4,12},{8,0},{12,4},{1,9},{5,13},{9,1},{13,5},{2,10},{6,14},... | collective-permute-start | bytes 1179656 | tf_op jit(solution)/shard_map/ppermute | solution.py:56
  18.1 18.9 %collective-permute-start.10 = (bf16[4,2,48,768]{3,2,1,0:T(8,128)(2,1)S(1)}, bf16[4,2,48,768]{3,2,1,0:T(8,128)(2,1)S(1)}, u32[]{:S(2)}, u32[]{:S(2)}) collective-permute-start(bf16[4,2,48,768]{3,2,1,0:T(8,128)(2,1)S(1)} %pad_maximum_fusion.5.s0), channel_id=1, source_target_pairs={{0,16},{16,0},{1,17},{17,1},{2,18},{18,2},{3,19},{19,3},{4,20},{20... | collective-permute-start | bytes 1769480 | tf_op jit(solution)/shard_map/ppermute | solution.py:56
  32.3 26.0 %collective-permute-start.9 = (bf16[4,2,48,768]{3,2,1,0:T(8,128)(2,1)S(1)}, bf16[4,2,48,768]{3,2,1,0:T(8,128)(2,1)S(1)}, u32[]{:S(2)}, u32[]{:S(2)}) collective-permute-start(bf16[4,2,48,768]{3,2,1,0:T(8,128)(2,1)S(1)} %pad_maximum_fusion.5.s0), channel_id=1, source_target_pairs={{0,4},{4,0},{8,12},{12,8},{1,5},{5,1},{9,13},{13,9},{2,6},{6,2},{1... | collective-permute-start | bytes 1769480 | tf_op jit(solution)/shard_map/ppermute | solution.py:56
  37.1 34.4 %collective-permute-start.11 = (bf16[4,2,48,768]{3,2,1,0:T(8,128)(2,1)S(1)}, bf16[4,2,48,768]{3,2,1,0:T(8,128)(2,1)S(1)}, u32[]{:S(2)}, u32[]{:S(2)}) collective-permute-start(bf16[4,2,48,768]{3,2,1,0:T(8,128)(2,1)S(1)} %collective-permute-done.10.s2), channel_id=1, source_target_pairs={{0,4},{4,0},{8,12},{12,8},{1,5},{5,1},{9,13},{13,9},{2,6},{6,2},{1... | collective-permute-start | bytes 1769480 | tf_op jit(solution)/shard_map/ppermute | solution.py:56
  55.5 24.3 %collective-permute-start.30 = (bf16[4,48,768]{2,1,0:T(8,128)(2,1)S(1)}, bf16[4,48,768]{2,1,0:T(8,128)(2,1)S(1)}, u32[]{:S(2)}, u32[]{:S(2)}) collective-permute-start(bf16[4,48,768]{2,1,0:T(8,128)(2,1)S(1)} %pad_maximum_fusion.10.refs_6_), channel_id=1, source_target_pairs={{0,4},{4,0},{8,12},{12,8},{1,5},{5,1},{9,13},{13,9},{2,6},{6,2},{1... | collective-permute-start | bytes 884744 | tf_op jit(solution)/shard_map/ppermute | solution.py:56
  69.6 22.9 %collective-permute-start.39 = (bf16[4,96,768]{2,1,0:T(8,128)(2,1)S(1)}, bf16[4,96,768]{2,1,0:T(8,128)(2,1)S(1)}, u32[]{:S(2)}, u32[]{:S(2)}) collective-permute-start(bf16[4,96,768]{2,1,0:T(8,128)(2,1)S(1)} %pad_maximum_fusion.6.refs_10_), channel_id=1, source_target_pairs={{0,16},{16,0},{1,17},{17,1},{2,18},{18,2},{3,19},{19,3},{4,20},{20... | collective-permute-start | bytes 1769480 | tf_op jit(solution)/shard_map/ppermute | solution.py:56
  80.6 41.8 %collective-permute-start.37 = (bf16[4,96,768]{2,1,0:T(8,128)(2,1)S(1)}, bf16[4,96,768]{2,1,0:T(8,128)(2,1)S(1)}, u32[]{:S(2)}, u32[]{:S(2)}) collective-permute-start(bf16[4,96,768]{2,1,0:T(8,128)(2,1)S(1)} %pad_maximum_fusion.6.refs_10_), channel_id=1, source_target_pairs={{0,8},{4,12},{8,0},{12,4},{1,9},{5,13},{9,1},{13,5},{2,10},{6,14},... | collective-permute-start | bytes 1769480 | tf_op jit(solution)/shard_map/ppermute | solution.py:56
  82.0 40.3 %collective-permute-start.47 = (bf16[4,96,768]{2,1,0:T(8,128)(2,1)S(1)}, bf16[4,96,768]{2,1,0:T(8,128)(2,1)S(1)}, u32[]{:S(2)}, u32[]{:S(2)}) collective-permute-start(bf16[4,96,768]{2,1,0:T(8,128)(2,1)S(1)} %pad_maximum_fusion.7.refs_18_), channel_id=1, source_target_pairs={{0,8},{4,12},{8,0},{12,4},{1,9},{5,13},{9,1},{13,5},{2,10},{6,14},... | collective-permute-start | bytes 1769480 | tf_op jit(solution)/shard_map/ppermute | solution.py:56
  84.2 38.7 %collective-permute-start.49 = (bf16[4,96,768]{2,1,0:T(8,128)(2,1)S(1)}, bf16[4,96,768]{2,1,0:T(8,128)(2,1)}, u32[]{:S(2)}, u32[]{:S(2)}) collective-permute-start(bf16[4,96,768]{2,1,0:T(8,128)(2,1)S(1)} %pad_maximum_fusion.7.refs_18_), channel_id=1, source_target_pairs={{0,16},{16,0},{1,17},{17,1},{2,18},{18,2},{3,19},{19,3},{4,20},{20... | collective-permute-start | bytes 1769480 | tf_op jit(solution)/shard_map/ppermute | solution.py:56
  86.3 24.4 %collective-permute-start.19 = (bf16[4,192,128]{2,1,0:T(8,128)(2,1)}, bf16[4,192,128]{2,1,0:T(8,128)(2,1)}, u32[]{:S(2)}, u32[]{:S(2)}) collective-permute-start(bf16[4,192,128]{2,1,0:T(8,128)(2,1)} %pad_maximum_fusion.17.q0), channel_id=1, source_target_pairs={{0,8},{4,12},{8,0},{12,4},{1,9},{5,13},{9,1},{13,5},{2,10},{6,14},... | collective-permute-start | bytes 589832 | tf_op jit(solution)/shard_map/ppermute | solution.py:56
  92.6 31.6 %collective-permute-start.18 = (bf16[4,192,128]{2,1,0:T(8,128)(2,1)}, bf16[4,192,128]{2,1,0:T(8,128)(2,1)S(1)}, u32[]{:S(2)}, u32[]{:S(2)}) collective-permute-start(bf16[4,192,128]{2,1,0:T(8,128)(2,1)} %pad_maximum_fusion.17.q0), channel_id=1, source_target_pairs={{0,4},{4,0},{8,12},{12,8},{1,5},{5,1},{9,13},{13,9},{2,6},{6,2},{1... | collective-permute-start | bytes 589832 | tf_op jit(solution)/shard_map/ppermute | solution.py:56
  122.4 18.9 %collective-permute-start.46 = (bf16[4,96,768]{2,1,0:T(8,128)(2,1)S(1)}, bf16[4,96,768]{2,1,0:T(8,128)(2,1)S(1)}, u32[]{:S(2)}, u32[]{:S(2)}) collective-permute-start(bf16[4,96,768]{2,1,0:T(8,128)(2,1)S(1)} %pad_maximum_fusion.7.refs_18_), channel_id=1, source_target_pairs={{0,4},{4,0},{8,12},{12,8},{1,5},{5,1},{9,13},{13,9},{2,6},{6,2},{1... | collective-permute-start | bytes 1769480 | tf_op jit(solution)/shard_map/ppermute | solution.py:56
  124.1 18.9 %collective-permute-start.51 = (bf16[4,96,768]{2,1,0:T(8,128)(2,1)S(1)}, bf16[4,96,768]{2,1,0:T(8,128)(2,1)}, u32[]{:S(2)}, u32[]{:S(2)}) collective-permute-start(bf16[4,96,768]{2,1,0:T(8,128)(2,1)S(1)} %collective-permute-done.47.refs_20_), channel_id=1, source_target_pairs={{0,16},{16,0},{1,17},{17,1},{2,18},{18,2},{3,19},{19,3},{4,20},{20... | collective-permute-start | bytes 1769480 | tf_op jit(solution)/shard_map/ppermute | solution.py:56
  124.4 18.8 %collective-permute-start.38 = (bf16[4,96,768]{2,1,0:T(8,128)(2,1)S(1)}, bf16[4,96,768]{2,1,0:T(8,128)(2,1)S(1)}, u32[]{:S(2)}, u32[]{:S(2)}) collective-permute-start(bf16[4,96,768]{2,1,0:T(8,128)(2,1)S(1)} %collective-permute-done.37.refs_12_), channel_id=1, source_target_pairs={{0,4},{4,0},{8,12},{12,8},{1,5},{5,1},{9,13},{13,9},{2,6},{6,2},{1... | collective-permute-start | bytes 1769480 | tf_op jit(solution)/shard_map/ppermute | solution.py:56
  159.9 20.7 %collective-permute-start.83 = (bf16[48,768]{1,0:T(8,128)(2,1)S(1)}, bf16[48,768]{1,0:T(8,128)(2,1)S(1)}, u32[]{:S(2)}, u32[]{:S(2)}) collective-permute-start(bf16[48,768]{1,0:T(8,128)(2,1)S(1)} %get-tuple-element.187), channel_id=1, source_target_pairs={{0,1},{1,0},{2,3},{3,2},{4,5},{5,4},{6,7},{7,6},{8,9},{9,8},{10,11... | collective-permute-start | bytes 221192 | tf_op jit(solution)/shard_map/ppermute | solution.py:56
  189.3 19.6 %collective-permute-start.59 = (bf16[4,208,128]{2,1,0:T(8,128)(2,1)S(1)}, bf16[4,208,128]{2,1,0:T(8,128)(2,1)S(1)}, u32[]{:S(2)}, u32[]{:S(2)}) collective-permute-start(bf16[4,208,128]{2,1,0:T(8,128)(2,1)S(1)} %pad_maximum_fusion.16.g0), channel_id=1, source_target_pairs={{0,4},{4,0},{8,12},{12,8},{1,5},{5,1},{9,13},{13,9},{2,6},{6,2},{1... | collective-permute-start | bytes 638984 | tf_op jit(solution)/shard_map/ppermute | solution.py:56
  194.5 85.8 %collective-permute-start.87 = (bf16[4,48,768]{2,1,0:T(8,128)(2,1)S(1)}, bf16[4,48,768]{2,1,0:T(8,128)(2,1)S(1)}, u32[]{:S(2)}, u32[]{:S(2)}) collective-permute-start(bf16[4,48,768]{2,1,0:T(8,128)(2,1)S(1)} %pad_maximum_fusion.11.s0), channel_id=1, source_target_pairs={{0,8},{4,12},{8,0},{12,4},{1,9},{5,13},{9,1},{13,5},{2,10},{6,14},... | collective-permute-start | bytes 884744 | tf_op jit(solution)/shard_map/ppermute | solution.py:56
  195.2 85.4 %collective-permute-start.91 = (bf16[4,48,768]{2,1,0:T(8,128)(2,1)S(1)}, bf16[4,48,768]{2,1,0:T(8,128)(2,1)S(1)}, u32[]{:S(2)}, u32[]{:S(2)}) collective-permute-start(bf16[4,48,768]{2,1,0:T(8,128)(2,1)S(1)} %collective-permute-done.89.s4), channel_id=1, source_target_pairs={{0,8},{4,12},{8,0},{12,4},{1,9},{5,13},{9,1},{13,5},{2,10},{6,14},... | collective-permute-start | bytes 884744 | tf_op jit(solution)/shard_map/ppermute | solution.py:56
  270.9 24.1 %collective-permute-start.86 = (bf16[4,48,768]{2,1,0:T(8,128)(2,1)S(1)}, bf16[4,48,768]{2,1,0:T(8,128)(2,1)S(1)}, u32[]{:S(2)}, u32[]{:S(2)}) collective-permute-start(bf16[4,48,768]{2,1,0:T(8,128)(2,1)S(1)} %pad_maximum_fusion.11.s0), channel_id=1, source_target_pairs={{0,4},{4,0},{8,12},{12,8},{1,5},{5,1},{9,13},{13,9},{2,6},{6,2},{1... | collective-permute-start | bytes 884744 | tf_op jit(solution)/shard_map/ppermute | solution.py:56
  272.1 72.1 %collective-permute-start.120 = (bf16[4,432,128]{2,1,0:T(8,128)(2,1)}, bf16[4,432,128]{2,1,0:T(8,128)(2,1)S(1)}, u32[]{:S(2)}, u32[]{:S(2)}) collective-permute-start(bf16[4,432,128]{2,1,0:T(8,128)(2,1)} %get-tuple-element.163), channel_id=1, source_target_pairs={{0,4},{4,0},{8,12},{12,8},{1,5},{5,1},{9,13},{13,9},{2,6},{6,2},{1... | collective-permute-start | bytes 1327112 | tf_op jit(solution)/shard_map/ppermute | solution.py:56
  283.9 57.1 %collective-permute-start.90 = (bf16[4,48,768]{2,1,0:T(8,128)(2,1)S(1)}, bf16[4,48,768]{2,1,0:T(8,128)(2,1)S(1)}, u32[]{:S(2)}, u32[]{:S(2)}) collective-permute-start(bf16[4,48,768]{2,1,0:T(8,128)(2,1)S(1)} %collective-permute-done.89.s4), channel_id=1, source_target_pairs={{0,4},{4,0},{8,12},{12,8},{1,5},{5,1},{9,13},{13,9},{2,6},{6,2},{1... | collective-permute-start | bytes 884744 | tf_op jit(solution)/shard_map/ppermute | solution.py:56
  285.1 54.9 %collective-permute-start.88 = (bf16[4,48,768]{2,1,0:T(8,128)(2,1)S(1)}, bf16[4,48,768]{2,1,0:T(8,128)(2,1)S(1)}, u32[]{:S(2)}, u32[]{:S(2)}) collective-permute-start(bf16[4,48,768]{2,1,0:T(8,128)(2,1)S(1)} %collective-permute-done.87.s2), channel_id=1, source_target_pairs={{0,4},{4,0},{8,12},{12,8},{1,5},{5,1},{9,13},{13,9},{2,6},{6,2},{1... | collective-permute-start | bytes 884744 | tf_op jit(solution)/shard_map/ppermute | solution.py:56
  288.4 55.4 %collective-permute-start.92 = (bf16[4,48,768]{2,1,0:T(8,128)(2,1)S(1)}, bf16[4,48,768]{2,1,0:T(8,128)(2,1)S(1)}, u32[]{:S(2)}, u32[]{:S(2)}) collective-permute-start(bf16[4,48,768]{2,1,0:T(8,128)(2,1)S(1)} %collective-permute-done.91.s6), channel_id=1, source_target_pairs={{0,4},{4,0},{8,12},{12,8},{1,5},{5,1},{9,13},{13,9},{2,6},{6,2},{1... | collective-permute-start | bytes 884744 | tf_op jit(solution)/shard_map/ppermute | solution.py:56
  295.7 50.4 %collective-permute-start.121 = (bf16[4,432,128]{2,1,0:T(8,128)(2,1)}, bf16[4,432,128]{2,1,0:T(8,128)(2,1)S(1)}, u32[]{:S(2)}, u32[]{:S(2)}) collective-permute-start(bf16[4,432,128]{2,1,0:T(8,128)(2,1)} %get-tuple-element.164), channel_id=1, source_target_pairs={{0,8},{4,12},{8,0},{12,4},{1,9},{5,13},{9,1},{13,5},{2,10},{6,14},... | collective-permute-start | bytes 1327112 | tf_op jit(solution)/shard_map/ppermute | solution.py:56
  340.0 42.2 %collective-permute-start.124 = (bf16[3,2,128,384]{3,2,1,0:T(8,128)(2,1)S(1)}, bf16[3,2,128,384]{3,2,1,0:T(8,128)(2,1)S(1)}, u32[]{:S(2)}, u32[]{:S(2)}) collective-permute-start(bf16[3,2,128,384]{3,2,1,0:T(8,128)(2,1)S(1)} %copy-done.26), channel_id=1, source_target_pairs={{0,8},{4,12},{8,0},{12,4},{1,9},{5,13},{9,1},{13,5},{2,10},{6,14},... | collective-permute-start | bytes 1769480 | tf_op jit(solution)/shard_map/ppermute | solution.py:56
  341.0 41.5 %collective-permute-start.123 = (bf16[3,2,128,384]{3,2,1,0:T(8,128)(2,1)S(1)}, bf16[3,2,128,384]{3,2,1,0:T(8,128)(2,1)S(1)}, u32[]{:S(2)}, u32[]{:S(2)}) collective-permute-start(bf16[3,2,128,384]{3,2,1,0:T(8,128)(2,1)S(1)} %copy-done.26), channel_id=1, source_target_pairs={{0,4},{4,0},{8,12},{12,8},{1,5},{5,1},{9,13},{13,9},{2,6},{6,2},{1... | collective-permute-start | bytes 1769480 | tf_op jit(solution)/shard_map/ppermute | solution.py:56
  343.8 20.8 %collective-permute-start.122 = (bf16[4,432,128]{2,1,0:T(8,128)(2,1)}, bf16[4,432,128]{2,1,0:T(8,128)(2,1)S(1)}, u32[]{:S(2)}, u32[]{:S(2)}) collective-permute-start(bf16[4,432,128]{2,1,0:T(8,128)(2,1)} %get-tuple-element.165), channel_id=1, source_target_pairs={{0,12},{4,8},{8,4},{12,0},{1,13},{5,9},{9,5},{13,1},{2,14},{6,10},... | collective-permute-start | bytes 1327112 | tf_op jit(solution)/shard_map/ppermute | solution.py:56
  344.2 44.8 %collective-permute-start.80 = (bf16[2,384,384]{2,1,0:T(8,128)(2,1)}, bf16[2,384,384]{2,1,0:T(8,128)(2,1)S(1)}, u32[]{:S(2)}, u32[]{:S(2)}) collective-permute-start(bf16[2,384,384]{2,1,0:T(8,128)(2,1)} %get-tuple-element.148.m1), channel_id=1, source_target_pairs={{0,1},{1,0},{2,3},{3,2},{4,5},{5,4},{6,7},{7,6},{8,9},{9,8},{10,11... | collective-permute-start | bytes 1769480 | tf_op jit(solution)/shard_map/ppermute | solution.py:56
  346.1 19.9 %collective-permute-start.68 = (bf16[192,128]{1,0:T(8,128)(2,1)}, bf16[192,128]{1,0:T(8,128)(2,1)S(1)}, u32[]{:S(2)}, u32[]{:S(2)}) collective-permute-start(bf16[192,128]{1,0:T(8,128)(2,1)} %get-tuple-element.135), channel_id=1, source_target_pairs={{0,1},{1,0},{2,3},{3,2},{4,5},{5,4},{6,7},{7,6},{8,9},{9,8},{10,11... | collective-permute-start | bytes 147464 | tf_op jit(solution)/shard_map/ppermute | solution.py:56
  386.5 40.2 %collective-permute-start.81 = (bf16[2,384,384]{2,1,0:T(8,128)(2,1)}, bf16[2,384,384]{2,1,0:T(8,128)(2,1)S(1)}, u32[]{:S(2)}, u32[]{:S(2)}) collective-permute-start(bf16[2,384,384]{2,1,0:T(8,128)(2,1)} %get-tuple-element.149.m2), channel_id=1, source_target_pairs={{0,2},{1,3},{2,0},{3,1},{4,6},{5,7},{6,4},{7,5},{8,10},{9,11},{10,... | collective-permute-start | bytes 1769480 | tf_op jit(solution)/shard_map/ppermute | solution.py:56
  389.0 51.0 %collective-permute-start.82 = (bf16[2,384,384]{2,1,0:T(8,128)(2,1)}, bf16[2,384,384]{2,1,0:T(8,128)(2,1)S(1)}, u32[]{:S(2)}, u32[]{:S(2)}) collective-permute-start(bf16[2,384,384]{2,1,0:T(8,128)(2,1)} %get-tuple-element.150.m3), channel_id=1, source_target_pairs={{0,3},{1,2},{2,1},{3,0},{4,7},{5,6},{6,5},{7,4},{8,11},{9,10},{10,... | collective-permute-start | bytes 1769480 | tf_op jit(solution)/shard_map/ppermute | solution.py:56
  389.0 51.8 %collective-permute-start.125 = (bf16[3,2,128,384]{3,2,1,0:T(8,128)(2,1)S(1)}, bf16[3,2,128,384]{3,2,1,0:T(8,128)(2,1)S(1)}, u32[]{:S(2)}, u32[]{:S(2)}) collective-permute-start(bf16[3,2,128,384]{3,2,1,0:T(8,128)(2,1)S(1)} %collective-permute-done.124.r2), channel_id=1, source_target_pairs={{0,4},{4,0},{8,12},{12,8},{1,5},{5,1},{9,13},{13,9},{2,6},{6,2},{1... | collective-permute-start | bytes 1769480 | tf_op jit(solution)/shard_map/ppermute | solution.py:56
  392.9 66.0 %collective-permute-start.103 = (bf16[2,2,128,384]{3,2,1,0:T(8,128)(2,1)}, bf16[2,2,128,384]{3,2,1,0:T(8,128)(2,1)S(1)}, u32[]{:S(2)}, u32[]{:S(2)}) collective-permute-start(bf16[2,2,128,384]{3,2,1,0:T(8,128)(2,1)} %get-tuple-element.158.r0), channel_id=1, source_target_pairs={{0,4},{4,0},{8,12},{12,8},{1,5},{5,1},{9,13},{13,9},{2,6},{6,2},{1... | collective-permute-start | bytes 1179656 | tf_op jit(solution)/shard_map/ppermute | solution.py:56
  394.1 64.8 %collective-permute-start.105 = (bf16[2,2,128,384]{3,2,1,0:T(8,128)(2,1)}, bf16[2,2,128,384]{3,2,1,0:T(8,128)(2,1)}, u32[]{:S(2)}, u32[]{:S(2)}) collective-permute-start(bf16[2,2,128,384]{3,2,1,0:T(8,128)(2,1)} %collective-permute-done.104.r2), channel_id=1, source_target_pairs={{0,4},{4,0},{8,12},{12,8},{1,5},{5,1},{9,13},{13,9},{2,6},{6,2},{1... | collective-permute-start | bytes 1179656 | tf_op jit(solution)/shard_map/ppermute | solution.py:56
  426.7 27.4 %collective-permute-start.101 = (bf16[4,96,128]{2,1,0:T(8,128)(2,1)S(1)}, bf16[4,96,128]{2,1,0:T(8,128)(2,1)S(1)}, u32[]{:S(2)}, u32[]{:S(2)}) collective-permute-start(bf16[4,96,128]{2,1,0:T(8,128)(2,1)S(1)} %copy-done.89), channel_id=1, source_target_pairs={{0,8},{4,12},{8,0},{12,4},{1,9},{5,13},{9,1},{13,5},{2,10},{6,14},... | collective-permute-start | bytes 294920 | tf_op jit(solution)/shard_map/ppermute | solution.py:56
  439.9 23.5 %collective-permute-start.71 = (bf16[2,384,256]{2,1,0:T(8,128)(2,1)S(1)}, bf16[2,384,256]{2,1,0:T(8,128)(2,1)S(1)}, u32[]{:S(2)}, u32[]{:S(2)}) collective-permute-start(bf16[2,384,256]{2,1,0:T(8,128)(2,1)S(1)} %copy-done.67), channel_id=1, source_target_pairs={{0,4},{4,0},{8,12},{12,8},{1,5},{5,1},{9,13},{13,9},{2,6},{6,2},{1... | collective-permute-start | bytes 1179656 | tf_op jit(solution)/shard_map/ppermute | solution.py:56
  440.8 22.7 %collective-permute-start.73 = (bf16[2,384,256]{2,1,0:T(8,128)(2,1)S(1)}, bf16[2,384,256]{2,1,0:T(8,128)(2,1)S(1)}, u32[]{:S(2)}, u32[]{:S(2)}) collective-permute-start(bf16[2,384,256]{2,1,0:T(8,128)(2,1)S(1)} %add_convert_fusion.1), channel_id=1, source_target_pairs={{0,8},{4,12},{8,0},{12,4},{1,9},{5,13},{9,1},{13,5},{2,10},{6,14},... | collective-permute-start | bytes 1179656 | tf_op jit(solution)/shard_map/ppermute | solution.py:56
  471.2 25.9 %collective-permute-start.93 = (bf16[2,144,384]{2,1,0:T(8,128)(2,1)}, bf16[2,144,384]{2,1,0:T(8,128)(2,1)}, u32[]{:S(2)}, u32[]{:S(2)}) collective-permute-start(bf16[2,144,384]{2,1,0:T(8,128)(2,1)} %get-tuple-element.180), channel_id=1, source_target_pairs={{0,4},{4,0},{8,12},{12,8},{1,5},{5,1},{9,13},{13,9},{2,6},{6,2},{1... | collective-permute-start | bytes 663560 | tf_op jit(solution)/shard_map/ppermute | solution.py:56
  471.5 25.6 %collective-permute-start.94 = (bf16[2,144,384]{2,1,0:T(8,128)(2,1)}, bf16[2,144,384]{2,1,0:T(8,128)(2,1)}, u32[]{:S(2)}, u32[]{:S(2)}) collective-permute-start(bf16[2,144,384]{2,1,0:T(8,128)(2,1)} %get-tuple-element.182), channel_id=1, source_target_pairs={{0,8},{4,12},{8,0},{12,4},{1,9},{5,13},{9,1},{13,5},{2,10},{6,14},... | collective-permute-start | bytes 663560 | tf_op jit(solution)/shard_map/ppermute | solution.py:56
  472.1 25.0 %collective-permute-start.95 = (bf16[2,144,384]{2,1,0:T(8,128)(2,1)}, bf16[2,144,384]{2,1,0:T(8,128)(2,1)}, u32[]{:S(2)}, u32[]{:S(2)}) collective-permute-start(bf16[2,144,384]{2,1,0:T(8,128)(2,1)} %get-tuple-element.181), channel_id=1, source_target_pairs={{0,12},{4,8},{8,4},{12,0},{1,13},{5,9},{9,5},{13,1},{2,14},{6,10},... | collective-permute-start | bytes 663560 | tf_op jit(solution)/shard_map/ppermute | solution.py:56
  490.6 72.3 %collective-permute-start.126 = (bf16[4,432,384]{2,1,0:T(8,128)(2,1)S(1)}, bf16[4,432,384]{2,1,0:T(8,128)(2,1)S(1)}, u32[]{:S(2)}, u32[]{:S(2)}) collective-permute-start(bf16[4,432,384]{2,1,0:T(8,128)(2,1)S(1)} %dynamic-slice_bitcast_fusion), channel_id=1, source_target_pairs={{0,16},{16,0},{1,17},{17,1},{2,18},{18,2},{3,19},{19,3},{4,20},{20... | collective-permute-start | bytes 3981320 | tf_op jit(solution)/shard_map/ppermute | solution.py:56
  493.8 32.3 %collective-permute-start.106 = (bf16[4,96,384]{2,1,0:T(8,128)(2,1)}, bf16[4,96,384]{2,1,0:T(8,128)(2,1)S(1)}, u32[]{:S(2)}, u32[]{:S(2)}) collective-permute-start(bf16[4,96,384]{2,1,0:T(8,128)(2,1)} %dynamic-slice_bitcast_fusion.1), channel_id=1, source_target_pairs={{0,16},{16,0},{1,17},{17,1},{2,18},{18,2},{3,19},{19,3},{4,20},{20... | collective-permute-start | bytes 884744 | tf_op jit(solution)/shard_map/ppermute | solution.py:56
  497.1 56.2 %collective-permute-start.77 = (bf16[128,768]{1,0:T(8,128)(2,1)}, bf16[128,768]{1,0:T(8,128)(2,1)}, u32[]{:S(2)}, u32[]{:S(2)}) collective-permute-start(bf16[128,768]{1,0:T(8,128)(2,1)} %add_parts.1.b0), channel_id=1, source_target_pairs={{0,1},{1,0},{2,3},{3,2},{4,5},{5,4},{6,7},{7,6},{8,9},{9,8},{10,11... | collective-permute-start | bytes 589832 | tf_op jit(solution)/shard_map/ppermute | solution.py:56
  530.3 28.4 %collective-permute-start.78 = (bf16[128,768]{1,0:T(8,128)(2,1)}, bf16[128,768]{1,0:T(8,128)(2,1)}, u32[]{:S(2)}, u32[]{:S(2)}) collective-permute-start(bf16[128,768]{1,0:T(8,128)(2,1)} %add_parts.1.b0), channel_id=1, source_target_pairs={{0,2},{1,3},{2,0},{3,1},{4,6},{5,7},{6,4},{7,5},{8,10},{9,11},{10,... | collective-permute-start | bytes 589832 | tf_op jit(solution)/shard_map/ppermute | solution.py:56
  532.9 25.8 %collective-permute-start.79 = (bf16[128,768]{1,0:T(8,128)(2,1)}, bf16[128,768]{1,0:T(8,128)(2,1)}, u32[]{:S(2)}, u32[]{:S(2)}) collective-permute-start(bf16[128,768]{1,0:T(8,128)(2,1)} %add_parts.1.b0), channel_id=1, source_target_pairs={{0,3},{1,2},{2,1},{3,0},{4,7},{5,6},{6,5},{7,4},{8,11},{9,10},{10,... | collective-permute-start | bytes 589832 | tf_op jit(solution)/shard_map/ppermute | solution.py:56
  558.7 37.3 %collective-permute-start.97 = (bf16[144,384]{1,0:T(8,128)(2,1)S(1)}, bf16[144,384]{1,0:T(8,128)(2,1)S(1)}, u32[]{:S(2)}, u32[]{:S(2)}) collective-permute-start(bf16[144,384]{1,0:T(8,128)(2,1)S(1)} %fusion.11), channel_id=1, source_target_pairs={{0,4},{4,0},{8,12},{12,8},{1,5},{5,1},{9,13},{13,9},{2,6},{6,2},{1... | collective-permute-start | bytes 331784 | tf_op jit(solution)/shard_map/ppermute | solution.py:56
  561.8 34.2 %collective-permute-start.99 = (bf16[144,384]{1,0:T(8,128)(2,1)S(1)}, bf16[144,384]{1,0:T(8,128)(2,1)S(1)}, u32[]{:S(2)}, u32[]{:S(2)}) collective-permute-start(bf16[144,384]{1,0:T(8,128)(2,1)S(1)} %collective-permute-done.98), channel_id=1, source_target_pairs={{0,4},{4,0},{8,12},{12,8},{1,5},{5,1},{9,13},{13,9},{2,6},{6,2},{1... | collective-permute-start | bytes 331784 | tf_op jit(solution)/shard_map/ppermute | solution.py:56
  565.3 29.5 %collective-permute-start.129 = (bf16[432,384]{1,0:T(8,128)(2,1)S(1)}, bf16[432,384]{1,0:T(8,128)(2,1)S(1)}, u32[]{:S(2)}, u32[]{:S(2)}) collective-permute-start(bf16[432,384]{1,0:T(8,128)(2,1)S(1)} %get-tuple-element.178), channel_id=1, source_target_pairs={{0,3},{1,2},{2,1},{3,0},{4,7},{5,6},{6,5},{7,4},{8,11},{9,10},{10,... | collective-permute-start | bytes 995336 | tf_op jit(solution)/shard_map/ppermute | solution.py:56
  (183 other events, 2079.0 us)
